TPU v7x, 256 devices: a whole 4x4x8 slice. The times are simulated.
256 devices in a mesh: row: 32 (over y, x, core), col: 8 (over z).
Axes of the slice: x: 4, y: 4, z: 8, core: 2. Of those that a mesh axis runs over, the one named last changes fastest.
Arguments:
- embeddings: bfloat16 [24576, 1024], P(('row', 'col')), may hold values from -8 to 8
- labels: int32 [24576], P(('row', 'col')), may hold values from 0 to 999
Outputs:
- grad: float32 [24576, 1024], P(('row', 'col'))
- loss: float32 [], replicated
All inputs are finite; a program needn't handle non-finite values.
Results may differ from a plain program's by a relative error of at most 0.0027.
Values may be sent and summed in bfloat16 or wider, within the bound.
A program may use at most 128 MiB of HBM per device.

v0:
```python
import jax
import jax.numpy as jnp
from jax import lax
from jax.sharding import PartitionSpec as P

LOGIT_HEAT_SCALE = 0.1
SHIFT = 10.0


def per_device(embeddings, labels):
    widened = embeddings.astype(jnp.float32)
    inverse = lax.rsqrt(jnp.sum(widened * widened, axis=1, keepdims=True) + 1e-06)
    unit_float = widened * inverse
    unit_length_embedding = unit_float.astype(jnp.bfloat16)
    own_count = unit_length_embedding.shape[0]
    col_size = lax.axis_size("col")
    row_size = lax.axis_size("row")
    row_index = lax.axis_index("row")
    col_index = lax.axis_index("col")
    reference_embedding_matrix, anchor_labels = (
        lax.all_gather(unit_length_embedding, "col", axis=0, tiled=True),
        lax.all_gather(labels, "col", axis=0, tiled=True),
    )
    anchor_count = reference_embedding_matrix.shape[0]
    anchor_index = row_index * anchor_count + jnp.arange(anchor_count, dtype=jnp.int32)
    key_vectors, key_labels = (
        lax.all_gather(unit_length_embedding, "row", axis=0, tiled=True),
        lax.all_gather(labels, "row", axis=0, tiled=True),
    )
    scaled_cosine_matrix = (
        jnp.dot(reference_embedding_matrix, key_vectors.T, preferred_element_type=jnp.float32)
        / LOGIT_HEAT_SCALE
    )
    key_count = key_labels.shape[0]
    position = jnp.arange(key_count, dtype=jnp.int32)
    key_index = (position // own_count * col_size + col_index) * own_count + position % own_count
    on_diagonal = anchor_index[:, None] == key_index[None, :]
    weights = jnp.where(on_diagonal, 0.0, jnp.exp(scaled_cosine_matrix - SHIFT))
    positive = jnp.where(
        (anchor_labels[:, None] == key_labels[None, :]) & ~on_diagonal, 1.0, 0.0
    ).astype(jnp.float32)
    exp_total, pos_total, pos_count = lax.psum(
        (
            jnp.sum(weights, axis=1),
            jnp.sum(positive * scaled_cosine_matrix, axis=1),
            jnp.sum(positive, axis=1),
        ),
        "col",
    )
    log_total = jnp.log(exp_total) + SHIFT
    divisor = jnp.maximum(pos_count, 1.0)
    anchor_loss = -(pos_total - pos_count * log_total) / divisor
    loss = lax.psum(jnp.sum(anchor_loss), "row") / (anchor_count * row_size)
    positive_match_factor = (weights / exp_total[:, None] - positive / divisor[:, None]).astype(
        jnp.bfloat16
    )
    mixers = (positive_match_factor,)
    mixer = mixers[0]
    source_side_derivative = jnp.dot(mixer, key_vectors, preferred_element_type=jnp.float32)
    source_side_derivative = source_side_derivative / LOGIT_HEAT_SCALE
    own_query = lax.psum_scatter(source_side_derivative, "col", scatter_dimension=0, tiled=True)
    cosine_inner_matrix = lax.dot_general(
        positive_match_factor,
        reference_embedding_matrix,
        (((0,), (0,)), ((), ())),
        preferred_element_type=jnp.float32,
    )
    self_key = lax.psum_scatter(
        cosine_inner_matrix / LOGIT_HEAT_SCALE, "row", scatter_dimension=0, tiled=True
    )
    unit_grad = own_query + self_key
    grad = (
        unit_grad - unit_float * jnp.sum(unit_float * unit_grad, axis=1, keepdims=True)
    ) * inverse
    return (grad, loss)


def solution(mesh):
    placed = (P(("row", "col"), None), P(("row", "col")))
    return jax.shard_map(
        per_device,
        mesh=mesh,
        in_specs=placed,
        out_specs=(P(("row", "col"), None), P()),
        check_vma=False,
    )
```

profile of v0, /device:TPU:1, one launch (start us, length us, event | category | flops | bytes accessed | tf_op | source)
XLA Modules:
  0.0 385.5 jit_solution(6043769614919583285)
XLA Ops:
  7.2 0.0 all-gather.3.cloned.1.call-start
  7.2 1.1 fusion.11
  8.3 1.7 fusion.7
  10.0 0.0 all-gather.5.cloned.1.call-start
  10.1 0.7 all-gather.5.cloned.1.call-update
  10.8 0.0 reduce-scatter.3.cloned.1.call-start
  10.8 1.3 dynamic-slice.1
  12.1 1.3 dynamic-slice
  14.7 0.9 dynamic-update-slice
  15.6 0.8 dynamic-update-slice.1
  16.4 14.2 %all-reduce = s32[768]{0:T(1024)S(1)} all-reduce(s32[768]{0:T(1024)S(1)} %dynamic-update-slice), channel_id=1, replica_groups=mesh['row'=32,'col'=8] {'col'}, use_global_device_ids=true, to_apply=%add | all-reduce | flops 768 | bytes 6144
  30.5 123.8 %all-reduce.1 = s32[3072]{0:T(1024)S(1)} all-reduce(s32[3072]{0:T(1024)S(1)} %dynamic-update-slice.1), channel_id=1, replica_groups=mesh['row'=32,'col'=8] {'row'}, use_global_device_ids=true, to_apply=%add.1 | all-reduce | flops 3072 | bytes 24576
  154.4 13.7 %fusion.2 = (f32[768]{0:T(1024)S(1)}, f32[768]{0:T(1024)S(1)}, f32[768]{0:T(1024)S(1)}, f32[768,3072]{1,0:T(8,128)}) fusion(s32[3072]{0:T(1024)S(1)} %fusion.21, s32[768]{0:T(1024)S(1)} %iota_add_fusion, s32[3072]{0:T(1024)S(1)} %all-reduce.1, s32[768]{0:T(1024)S(1)} %all-reduce, bf16[768,1024]{1,0:T(8,128)(2,1)} %all-gather.3.cloned.1.call-done, ...), kind=kOutput, calls=%fused_computation.7 | convolution fusion | flops 4860146688 | bytes 17341440 | tf_op jit(solution)/shard_map/dot_general | solution.py:31
  168.1 20.7 %all-reduce.2 = (f32[768]{0:T(1024)S(1)}, f32[768]{0:T(1024)S(1)}, f32[768]{0:T(1024)S(1)}) all-reduce(f32[768]{0:T(1024)S(1)} %get-tuple-element.4, f32[768]{0:T(1024)S(1)} %get-tuple-element.3, f32[768]{0:T(1024)S(1)} %get-tuple-element.2), channel_id=1, replica_groups=mesh['row'=32,'col'=8] {'col'}, use_global_device_ids=true, to_apply=%region_4.5 | all-reduce | flops 2304 | bytes 18432 | tf_op jit(solution)/shard_map/psum | solution.py:42
  188.8 0.6 divide_reduce_fusion
  189.4 7.8 %fusion.1 = bf16[768,3072]{1,0:T(8,128)(2,1)S(1)} fusion(f32[768,3072]{1,0:T(8,128)} %get-tuple-element.12, f32[768]{0:T(1024)S(1)} %get-tuple-element.11, f32[768]{0:T(1024)S(1)} %get-tuple-element.6, s32[3072]{0:T(1024)S(1)} %fusion.21, s32[768]{0:T(1024)S(1)} %iota_add_fusion, s32[3072]{0:T(1024)S(1)} %all-reduce.1, s32[768]{0:T(1024)S(1)} %all-reduce), kind=kLoop, calls=%fused_computation.6 | loop fusion | flops 28311552 | bytes 14192640 | tf_op jit(solution)/shard_map/convert_element_type | solution.py:54
  197.3 2.1 copy-done
  199.4 8.4 %convolution_multiply_fusion.1 = f32[768,1024]{1,0:T(8,128)} fusion(bf16[768,3072]{1,0:T(8,128)(2,1)S(1)} %fusion.1, bf16[3072,1024]{1,0:T(8,128)(2,1)} %all-gather.5.cloned.1.call-done), kind=kOutput, calls=%fused_computation.11 | convolution fusion | flops 4832624640 | bytes 14155776 | tf_op jit(solution)/shard_map/dot_general | solution.py:59
  207.8 0.2 reduce-scatter.5.cloned.1.call-start
  208.1 10.4 %convolution_multiply_fusion = f32[3072,1024]{1,0:T(8,128)} fusion(bf16[768,3072]{1,0:T(8,128)(2,1)} %copy-done, bf16[768,1024]{1,0:T(8,128)(2,1)S(1)} %copy-done.2), kind=kOutput, calls=%fused_computation.10 | convolution fusion | flops 4834983936 | bytes 18874368 | tf_op jit(solution)/shard_map/dot_general | solution.py:62
  218.5 75.4 %psum.31 = f32[]{:T(128)} all-reduce(f32[]{:T(128)} %get-tuple-element.10), channel_id=1, replica_groups=mesh['row'=32,'col'=8] {'row'}, use_global_device_ids=true, to_apply=%region_11.12 | all-reduce | flops 1 | bytes 8 | tf_op jit(solution)/shard_map/psum | solution.py:53
  294.5 81.0 %reduce-scatter.5.cloned.1.call-done = f32[96,1024]{1,0:T(8,128)} async-done(((f32[3072,1024]{1,0:T(8,128)}), f32[96,1024]{1,0:T(8,128)}) %reduce-scatter.5.cloned.1.call-update) | async-done | bytes 393232 | tf_op jit(solution)/shard_map/reduce_scatter | solution.py:68
  375.6 1.3 fusion.8
  376.9 0.9 fusion.10
  (16 shorter events, 0.1 us)
Async XLA Ops:
  7.2 147.2 %all-gather.3.cloned.1.call-start = ((), (), s32[]{:S(2)}) async-start(), calls=%async_computation.2 | async-start | bytes 1769472 | tf_op jit(solution)/shard_map/all_gather | solution.py:21
  10.0 144.4 %all-gather.5.cloned.1.call-start = ((), (), s32[]{:S(2)}) async-start(), calls=%async_computation.3 | async-start | bytes 6488064 | tf_op jit(solution)/shard_map/all_gather | solution.py:27
  10.8 283.8 %reduce-scatter.3.cloned.1.call-start = ((), (), s32[]{:S(2)}) async-start(), calls=%async_computation.4 | async-start | bytes 3538944 | tf_op jit(solution)/shard_map/reduce_scatter | solution.py:61
  197.3 2.1 copy-start
  199.4 8.7 %copy-start.2 = (bf16[768,1024]{1,0:T(8,128)(2,1)S(1)}, bf16[768,1024]{1,0:T(8,128)(2,1)}, u32[]{:S(2)}) copy-start(bf16[768,1024]{1,0:T(8,128)(2,1)} %all-gather.3.cloned.1.call-done) | copy-start | bytes 4718596
  207.8 167.8 %reduce-scatter.5.cloned.1.call-start = ((), (), s32[]{:S(2)}) async-start(), calls=%async_computation.5 | async-start | bytes 12976128 | tf_op jit(solution)/shard_map/reduce_scatter | solution.py:68
  218.5 157.1 %copy-start.1 = (bf16[96,1024]{1,0:T(8,128)(2,1)S(1)}, bf16[96,1024]{1,0:T(8,128)(2,1)}, u32[]{:S(2)}) copy-start(bf16[96,1024]{1,0:T(8,128)(2,1)} %param.2) | copy-start | bytes 589828
Sparse Core Ops, SparseCore 0:
  10.4 40.0 all-gather.2
  53.5 57.0 all-gather.4
  208.0 50.7 reduce-scatter.2
  262.7 112.8 reduce-scatter.4
where the time goes:
time: 386 us
  blocking collectives  234 us (61%)
  waiting for transfers between devices  81.8 us (21%)
  matrix products  32.5 us (8%)
  between operations  16.9 us (4%)
  other arithmetic  13.5 us (3%)
  local copies, waits for them, and re-layouts  6.37 us (2%)
    unnamed x2, blocking collectives  138 us
    reduce_scatter x1, waiting for transfers between devices, per_device(): lax.psum_scatter(cosine_inner_matrix / LOGIT_HEAT_SCALE, 'row', scatter_d...  81 us
    psum x1, blocking collectives, per_device(): loss = lax.psum(jnp.sum(anchor_loss), 'row') / (anchor_count * row_size)  75.4 us
    psum x1, blocking collectives, per_device(): lax.psum((jnp.sum(weights, axis=1), jnp.sum(positive * scaled_cosine_matr...  20.7 us
    dot_general x1, matrix products, per_device(): jnp.dot(reference_embedding_matrix, key_vectors.T, preferred_element_type...  13.7 us
    dot_general x1, matrix products, per_device(): lax.dot_general(positive_match_factor, reference_embedding_matrix, (((0,)...  10.4 us
    dot_general x1, matrix products, per_device(): jnp.dot(mixer, key_vectors, preferred_element_type=jnp.float32)  8.44 us
    convert_element_type x1, other arithmetic, per_device(): (weights / exp_total[:, None] - positive / divisor[:, None]).astype(jnp.b...  7.84 us
  transfers between devices with their start and end apart: 4, of which 1 were waited for; matrix products, arithmetic and copies ran while one was open for 4% of the time, Pallas kernels for 0%

commit v1 on v0

v1 whole, which is shorter than its diff:
```python
import jax
import jax.numpy as jnp
from jax import lax
from jax.experimental import pallas as pl
from jax.experimental.pallas import tpu as pltpu
from jax.sharding import PartitionSpec as P

F32 = jnp.float32
BF16 = jnp.bfloat16
MESH = pl.DeviceIdType.MESH
LOG2E = 1.4426950408889634
NT = (((1,), (1,)), ((), ()))

BLOCK = 96
HALF = 48
DEPTH = 1024
N_Z = 8
ANCHORS = N_Z * BLOCK
KEYS = 32 * BLOCK
GROUP = 8 * BLOCK
CHUNKS = 4
WIDE = DEPTH // CHUNKS
TOKENS = 24576

A_POS = {0: 0, 7: 1, 1: 2, 6: 3, 2: 4, 5: 5, 3: 6, 4: 7}
K_ORDER = [
    (0, 0), (0, 3), (0, 1), (3, 0),
    (1, 0), (0, 2), (3, 3), (1, 3),
    (3, 1), (1, 1), (2, 0), (3, 2),
    (1, 2), (2, 3), (2, 1), (2, 2),
]
K_POS = {d: i for i, d in enumerate(K_ORDER)}
SHIFTS = (0, 96, 64, 32)
ARRIVALS = [
    ("A", 7, 0), ("A", 1, 0), ("K", 0, 3, 0), ("K", 0, 1, 0), ("K", 3, 0, 0), ("K", 1, 0, 0),
    ("A", 7, 1), ("A", 1, 1), ("K", 0, 3, 1), ("K", 0, 1, 1), ("K", 3, 0, 1), ("K", 1, 0, 1),
    ("K", 0, 2, 0), ("K", 0, 2, 1), ("A", 6, 0), ("A", 2, 0), ("K", 3, 3, 0), ("K", 1, 3, 0),
    ("A", 6, 1), ("A", 2, 1), ("K", 3, 1, 0), ("K", 1, 1, 0), ("K", 3, 3, 1), ("K", 1, 3, 1),
    ("K", 2, 0, 0), ("K", 3, 1, 1), ("K", 1, 1, 1), ("K", 2, 0, 1),
    ("A", 5, 0), ("A", 3, 0), ("A", 5, 1), ("A", 3, 1), ("K", 3, 2, 0), ("K", 1, 2, 0),
    ("K", 2, 3, 0), ("K", 3, 2, 1), ("K", 1, 2, 1), ("K", 2, 3, 1),
    ("A", 4, 0), ("A", 4, 1), ("K", 2, 1, 0), ("K", 2, 1, 1), ("K", 2, 2, 0), ("K", 2, 2, 1),
]


def key_row(core, dq, dp):
    q = K_POS[(dq, dp)]
    return (q // 4) * GROUP + core * (GROUP // 2) + (q % 4) * BLOCK


def key_slot(core, dq, dp):
    return core * 16 + K_POS[(dq, dp)]


class Semaphores:
    def __init__(self):
        self.numbers = {}

    def __call__(self, name):
        return self.numbers.setdefault(name, len(self.numbers))


N_SEM = 260


def kernel(emb, lab, grad, loss,
           au, ku, w, cm, g, uf, inv,
           var, al, kl, labc, klab,
           est, pst, cst, s1o, s1i, s2o, s2i, iec, idc, kev, ke, kie,
           lo, li, sb, rb, send, recv):
    row, z = lax.axis_index("row"), lax.axis_index("col")
    core, x, y = row % 2, (row // 2) % 4, row // 8
    number = Semaphores()
    pending = []

    def chip(dp, dq, other):
        px = (x + dp + core * (dq - dp) + 8) % 4
        py = (y + dq + core * (dp - dq) + 8) % 4
        pc = 1 - core if other else core
        return ((py * 4 + px) * 2 + pc, z)

    def up(dz):
        return (row, (z + dz + 8) % 8)

    def message(name, src, dst, to):
        i = number(name)
        return pltpu.make_async_remote_copy(
            src_ref=src, dst_ref=dst, send_sem=send.at[i], recv_sem=recv.at[i], device_id=to, device_id_type=MESH
        )

    def post(name, src, dst, to):
        copy = message(name, src, dst, to)
        copy.start()
        pending.append(copy)

    def arrived(name, dst):
        message(name, dst, dst, up(1)).wait_recv()

    def a_ref(dz, h):
        return au.at[pl.ds(A_POS[dz] * BLOCK + h * HALF, HALF), :]

    def k_ref(s, dq, dp, h):
        return ku.at[pl.ds(key_row(s, dq, dp) + h * HALF, HALF), :]

    peers = [(s, dq, dp) for s in (0, 1) for dq, dp in K_ORDER if (s, dq, dp) != (0, 0, 0)]

    barrier = pltpu.get_barrier_semaphore()
    for dz in range(1, N_Z):
        pl.semaphore_signal(barrier, inc=1, device_id=up(dz), device_id_type=MESH)
    for s, dq, dp in peers:
        pl.semaphore_signal(barrier, inc=1, device_id=chip(-dp, -dq, s), device_id_type=MESH)

    wide = emb[...].astype(F32)
    scale = lax.rsqrt(jnp.sum(wide * wide, axis=1, keepdims=True) + 1e-6)
    unit = wide * scale
    uf[...] = unit
    inv[...] = jnp.broadcast_to(scale, (BLOCK, 128))
    own = unit.astype(BF16)
    au[pl.ds(0, BLOCK), :] = own
    ku[pl.ds(0, BLOCK), :] = own
    own_label = lab[...].astype(F32)
    al[0] = own_label
    for p, shift in enumerate(SHIFTS):
        var[p] = pltpu.roll(own_label, shift, 1) if shift else own_label
    kl[0] = own_label
    est[...] = jnp.zeros_like(est)
    pst[...] = jnp.zeros_like(pst)
    cst[...] = jnp.zeros_like(cst)
    pl.semaphore_wait(barrier, N_Z - 1 + len(peers))

    def hand_on(what):
        if what[0] == "A":
            _, dz, h = what
            if dz == 0:
                ways = ((1, 7), (-1, 1))
            elif dz in (7, 6) or (dz == 5 and h == 0):
                ways = ((1, dz - 1),)
            elif dz in (1, 2) or (dz == 3 and h == 1):
                ways = ((-1, dz + 1),)
            else:
                ways = ()
            for step, there in ways:
                post(("A", there, h), a_ref(dz, h), a_ref(there, h), up(step))
            return
        _, dq, dp, h = what
        src = k_ref(0, dq, dp, h)
        ways = []
        if dq == 0:
            if dp == 0:
                ways += [(1, 0, 0, 3), (-1, 0, 0, 1)]
            elif dp == 3 and h == 0:
                ways += [(1, 0, 0, 2)]
            elif dp == 1 and h == 1:
                ways += [(-1, 0, 0, 2)]
            ways += [(0, 1, 3, dp), (0, -1, 1, dp)]
        elif dq == 3 and h == 0:
            ways += [(0, 1, 2, dp)]
        elif dq == 1 and h == 1:
            ways += [(0, -1, 2, dp)]
        for tp, tq, nq, np_ in ways:
            post(("K", nq, np_, h), src, k_ref(0, nq, np_, h), chip(tp, tq, False))
        post(("S", dq, dp, h), src, k_ref(1, dq, dp, h), chip(0, 0, True))

    for h in (0, 1):
        hand_on(("A", 0, h))
        hand_on(("K", 0, 0, h))
    for dz in range(1, N_Z):
        post(("L", 8 - dz), al.at[0], al.at[8 - dz], up(dz))
    for s, dq, dp in peers:
        post(("M", s, dq, dp), var.at[K_POS[(dq, dp)] % 4], kl.at[key_slot(s, dq, dp)], chip(-dp, -dq, s))

    lane = lax.broadcasted_iota(jnp.int32, (1, 128), 1)

    def columns(rows):
        stack = jnp.concatenate(list(rows) + [jnp.zeros((128 - N_Z, 128), F32)], axis=0)
        turned = jnp.transpose(stack)
        return [jnp.broadcast_to(turned[:BLOCK, p : p + 1], (BLOCK, 128)) for p in range(N_Z)]

    def key_line(slots, out):
        for s in (0, 1):
            for q in range(4):
                m = [slots[s * 16 + q * 4 + p] for p in range(4)]
                base = q * GROUP + s * (GROUP // 2)
                for t, (cut, a, b) in enumerate(((96, 0, 1), (64, 1, 2), (32, 2, 3))):
                    line = jnp.where(lane < cut, m[a], m[b])
                    out[:, pl.ds(base + t * 128, 128)] = jnp.broadcast_to(line, (8, 128))

    def labels_ready():
        for dz in range(1, N_Z):
            arrived(("L", dz), al.at[dz])
        for s, dq, dp in peers:
            arrived(("M", s, dq, dp), kl.at[key_slot(s, dq, dp)])
        by_pos = sorted(A_POS, key=A_POS.get)
        for p, block in enumerate(columns([al[dz] for dz in by_pos])):
            labc[pl.ds(p * BLOCK, BLOCK), :] = block
        key_line(kl, klab)

    def on_diagonal(rows):
        r = lax.broadcasted_iota(jnp.int32, (rows, 128), 0)
        c = lax.broadcasted_iota(jnp.int32, (rows, 128), 1)
        return (r == c) & (r < BLOCK)

    def score(r0, rows, c0, cols):
        at = pl.ds(r0, rows)
        acc = lax.dot_general(au[at, :], ku[pl.ds(c0, cols), :], NT, preferred_element_type=F32)
        label = labc[at, :]
        total = positive = count = None
        for t in range(cols // 128):
            here = pl.ds(c0 + t * 128, 128)
            s = acc[:, t * 128 : (t + 1) * 128]
            e = jnp.exp2(s * (10.0 * LOG2E) - 10.0 * LOG2E)
            same = label == klab[0:1, here]
            if r0 == 0 and c0 + t == 0:
                diagonal = on_diagonal(rows)
                e = jnp.where(diagonal, 0.0, e)
                same = same & ~diagonal
            w[at, here] = e
            ps, cs = jnp.where(same, s, 0.0), jnp.where(same, 1.0, 0.0)
            if t == 0:
                total, positive, count = e, ps, cs
            else:
                total, positive, count = total + e, positive + ps, count + cs
        est[at, :] += total
        pst[at, :] += positive
        cst[at, :] += count

    def need(r0, rows, c0, cols):
        wants = set()
        for dz, p in A_POS.items():
            if dz and p * BLOCK < r0 + rows and (p + 1) * BLOCK > r0:
                wants |= {("A", dz, 0), ("A", dz, 1)}
        for s in (0, 1):
            for dq, dp in K_ORDER:
                k0 = key_row(s, dq, dp)
                if k0 < c0 + cols and k0 + BLOCK > c0 and (s, dq, dp) != (0, 0, 0):
                    wants |= {("S" if s else "K", dq, dp, h) for h in (0, 1)}
        return wants

    work = []
    for c in range(0, GROUP, 256):
        work.append((0, 480, c, 256))
    for c in range(0, GROUP, 256):
        work.append((0, 480, GROUP + c, 256))
    for c in range(0, 2 * GROUP, 256):
        work.append((480, 288, c, 256))
    for c in range(0, GROUP, 256):
        work.append((0, 768, 2 * GROUP + c, 256))
    for c in range(0, GROUP, 256):
        work.append((0, 768, 3 * GROUP + c, 256))

    seen = set()

    def receive(what):
        if what in seen:
            return
        seen.add(what)
        if what[0] == "A":
            arrived(what, a_ref(what[1], what[2]))
        else:
            arrived(what, k_ref(1 if what[0] == "S" else 0, *what[1:]))
        if what[0] != "S":
            hand_on(what)

    def can_run(wants):
        return all(v in seen for v in wants if v[0] != "S")

    ready = False
    for n, what in enumerate(ARRIVALS):
        receive(what)
        if n == 11:
            labels_ready()
            ready = True
        if ready and work and n < len(ARRIVALS) - 1:
            wants = need(*work[0])
            if can_run(wants) and all(("K",) + v[1:] in set(ARRIVALS[: max(n - 5, 0)]) | {("K", 0, 0, 0), ("K", 0, 0, 1)}
                                      for v in wants if v[0] == "S"):
                for v in sorted(wants - seen):
                    receive(v)
                score(*work.pop(0))
    for job in work:
        for v in sorted(need(*job) - seen):
            receive(v)
        score(*job)

    for dz in (4, 3, 5, 2, 6, 1, 7, 0):
        for i, stat in enumerate((est, pst, cst)):
            part = jnp.transpose(stat[pl.ds(A_POS[dz] * BLOCK, 128), :])
            s1o[dz, i : i + 1, :] = jnp.sum(part, axis=0, keepdims=True)
        if dz:
            post(("T", 8 - dz), s1o.at[dz], s1i.at[8 - dz], up(dz))
    sums = s1o[0]
    for dz in range(1, N_Z):
        arrived(("T", dz), s1i.at[dz])
        sums = sums + s1i[dz]
    real = lane < BLOCK
    exp_total = jnp.where(real, sums[0:1], 1.0)
    pos_total = jnp.where(real, sums[1:2], 0.0) * 10.0
    pos_count = jnp.where(real, sums[2:3], 0.0)
    divisor = jnp.maximum(pos_count, 1.0)
    anchor_loss = -(pos_total - pos_count * (jnp.log(exp_total) + 10.0)) / divisor
    inverse_total = 1.0 / exp_total
    s2o[0:1, :] = inverse_total
    s2o[1:2, :] = 2.0 / divisor
    s2o[2:3, :] = jnp.where(real, anchor_loss, 0.0)
    s2o[3:4, :] = jnp.zeros((1, 128), F32)
    s2i[0] = s2o[...]
    for p, shift in enumerate(SHIFTS):
        kev[p] = pltpu.roll(inverse_total, shift, 1) if shift else inverse_total
    ke[0] = inverse_total
    for dz in range(1, N_Z):
        post(("U", 8 - dz), s2o, s2i.at[8 - dz], up(dz))
    for s, dq, dp in peers:
        post(("V", s, dq, dp), kev.at[K_POS[(dq, dp)] % 4], ke.at[key_slot(s, dq, dp)], chip(-dp, -dq, s))
    for dz in range(1, N_Z):
        arrived(("U", dz), s2i.at[dz])
    by_pos = sorted(A_POS, key=A_POS.get)
    for p, block in enumerate(columns([s2i[dz, 0:1, :] for dz in by_pos])):
        iec[pl.ds(p * BLOCK, BLOCK), :] = block
    for p, block in enumerate(columns([s2i[dz, 1:2, :] for dz in by_pos])):
        idc[pl.ds(p * BLOCK, BLOCK), :] = block
    lo[...] = sum(s2i[dz, 2:3, :] for dz in range(N_Z))
    for s, dq, dp in peers:
        arrived(("V", s, dq, dp), ke.at[key_slot(s, dq, dp)])
    key_line(ke, kie)

    def coupling(c0):
        for r in range(0, ANCHORS, 16):
            at = pl.ds(r, 16)
            ie, d2, label = iec[at, :], idc[at, :], labc[at, :]
            for t in range(GROUP // 128):
                here = pl.ds(c0 + t * 128, 128)
                same = label == klab[0:1, here]
                if c0 + t == 0 and r < BLOCK:
                    i = lax.broadcasted_iota(jnp.int32, (16, 128), 0) + r
                    same = same & (i != lax.broadcasted_iota(jnp.int32, (16, 128), 1))
                v = w[at, here] * (ie + kie[0:1, here]) - jnp.where(same, d2, 0.0)
                cm[at, here] = v.astype(BF16)

    def part(j, dz, lo_, n):
        return g[j, pl.ds(A_POS[dz] * BLOCK + lo_, n), :]

    def push(j, step):
        for way, sign in enumerate((1, -1)):
            dz = (sign * (4 - step)) % 8
            if step == 0:
                at, n = way * HALF, HALF
                value = part(j, dz, at, n)
            else:
                at, n = 0, BLOCK
                value = part(j, dz, 0, BLOCK)
                if step == 1:
                    got = slice(way * HALF, (way + 1) * HALF)
                    arrived(("R", j, way, 0), rb.at[j, way, 0, pl.ds(way * HALF, HALF), :])
                    far = rb[j, way, 0, got, :].astype(F32)
                    pieces = [value[:HALF], value[HALF:]]
                    pieces[way] = pieces[way] + far
                    value = jnp.concatenate(pieces, axis=0)
                else:
                    arrived(("R", j, way, step - 1), rb.at[j, way, step - 1])
                    value = value + rb[j, way, step - 1].astype(F32)
            sb[j, way, step, at : at + n, :] = value.astype(BF16)
            rows = pl.ds(at, n)
            post(("R", j, way, step), sb.at[j, way, step, rows, :], rb.at[j, way, step, rows, :], up(sign))

    def product(j):
        g[j] = jnp.dot(cm[...], ku[:, j * WIDE : (j + 1) * WIDE], preferred_element_type=F32)

    for q in range(4):
        coupling(q * GROUP)
    for n in range(CHUNKS + 3):
        if n < CHUNKS:
            product(n)
            push(n, 0)
        for j in range(min(n - 1, CHUNKS - 1), -1, -1):
            if 0 < n - j < 4:
                push(j, n - j)
        if n == 1:
            for s, dq, dp in peers:
                post(("W", s, dq, dp), lo, li.at[key_slot(s, dq, dp)], chip(-dp, -dq, s))

    every = lo[...]
    for s, dq, dp in peers:
        arrived(("W", s, dq, dp), li.at[key_slot(s, dq, dp)])
        every = every + li[key_slot(s, dq, dp)]
    loss[...] = jnp.broadcast_to(jnp.sum(every, axis=1, keepdims=True) * (1.0 / TOKENS), (1, 128))

    for j in range(CHUNKS):
        value = part(j, 0, 0, BLOCK)
        for way in (0, 1):
            arrived(("R", j, way, 3), rb.at[j, way, 3])
            value = value + rb[j, way, 3].astype(F32)
        g[j, pl.ds(0, BLOCK), :] = value * 10.0
    along = jnp.zeros((BLOCK, 1), F32)
    for j in range(CHUNKS):
        cut = slice(j * WIDE, (j + 1) * WIDE)
        along = along + jnp.sum(uf[:, cut] * g[j, pl.ds(0, BLOCK), :], axis=1, keepdims=True)
    scale = inv[:, 0:1]
    for j in range(CHUNKS):
        cut = slice(j * WIDE, (j + 1) * WIDE)
        grad[:, cut] = (g[j, pl.ds(0, BLOCK), :] - uf[:, cut] * along) * scale

    for copy in pending:
        copy.wait_send()
    assert len(number.numbers) <= N_SEM


def per_device(embeddings, labels):
    vmem = pl.BlockSpec(memory_space=pltpu.VMEM)
    line = jnp.pad(labels, (0, 128 - BLOCK)).reshape(1, 128)
    scratch = [
        ((ANCHORS, DEPTH), BF16),
        ((KEYS, DEPTH), BF16),
        ((ANCHORS, KEYS), F32),
        ((ANCHORS, KEYS), BF16),
        ((CHUNKS, ANCHORS, WIDE), F32),
        ((BLOCK, DEPTH), F32),
        ((BLOCK, 128), F32),
        ((4, 1, 128), F32),
        ((N_Z, 1, 128), F32),
        ((32, 1, 128), F32),
        ((ANCHORS, 128), F32),
        ((8, KEYS), F32),
        ((ANCHORS + 32, 128), F32),
        ((ANCHORS + 32, 128), F32),
        ((ANCHORS + 32, 128), F32),
        ((N_Z, 4, 128), F32),
        ((N_Z, 4, 128), F32),
        ((4, 128), F32),
        ((N_Z, 4, 128), F32),
        ((ANCHORS, 128), F32),
        ((ANCHORS, 128), F32),
        ((4, 1, 128), F32),
        ((32, 1, 128), F32),
        ((8, KEYS), F32),
        ((1, 128), F32),
        ((32, 1, 128), F32),
        ((CHUNKS, 2, 4, BLOCK, WIDE), BF16),
        ((CHUNKS, 2, 4, BLOCK, WIDE), BF16),
    ]
    grad, loss = pl.pallas_call(
        kernel,
        out_shape=(
            jax.ShapeDtypeStruct((BLOCK, DEPTH), F32),
            jax.ShapeDtypeStruct((1, 128), F32),
        ),
        in_specs=[vmem, vmem],
        out_specs=(vmem, vmem),
        scratch_shapes=[pltpu.VMEM(s, t) for s, t in scratch]
        + [pltpu.SemaphoreType.DMA((N_SEM,)), pltpu.SemaphoreType.DMA((N_SEM,))],
        compiler_params=pltpu.CompilerParams(
            collective_id=0, has_side_effects=True, vmem_limit_bytes=60 * 2**20
        ),
        cost_estimate=pl.CostEstimate(flops=2 * 2 * ANCHORS * KEYS * DEPTH, bytes_accessed=2**20, transcendentals=0),
    )(embeddings, line)
    return grad, loss[0, 0]


def solution(mesh):
    placed = (P(("row", "col"), None), P(("row", "col")))
    return jax.shard_map(
        per_device,
        mesh=mesh,
        in_specs=placed,
        out_specs=(P(("row", "col"), None), P()),
        check_vma=False,
    )
```

time: 386 us -> 86.9 us (0.23)
  the two profiles are of different devices: /device:TPU:1 before, /device:TPU:6 now
where the time goes in v1:
time: 86.9 us; the launch traced here: 86.8 us
  Pallas kernels  82 us (94%)
  local copies, waits for them, and re-layouts  2.94 us (3%)
  between operations  1.81 us (2%)
    pallas_call x1, Pallas kernels, per_device(): pl.pallas_call(kernel, out_shape=(jax.ShapeDtypeStruct((BLOCK, DEPTH), F3...  82 us
    unnamed x3, local copies, waits for them, and re-layouts  1.77 us

profile of v1, /device:TPU:6, one launch (start us, length us, event | category | flops | bytes accessed | tf_op | source)
XLA Modules:
  0.0 86.8 jit_solution(7150412314359599187)
XLA Ops:
  0.6 1.2 %pad_bitcast_fusion.lab = s32[1,128]{1,0:T(1,128)} fusion(s32[96]{0:T(128)} %param.3), kind=kLoop, calls=%fused_computation | loop fusion | bytes 896 | tf_op jit(solution)/shard_map/reshape | solution.py:409
  1.8 82.0 %shard_map.41 = (f32[96,1024]{1,0:T(8,128)}, f32[1,128]{1,0:T(1,128)}) custom-call(bf16[96,1024]{1,0:T(8,128)(2,1)} %emb.1, s32[1,128]{1,0:T(1,128)} %pad_bitcast_fusion.lab), custom_call_target="tpu_custom_call" | custom-call | flops 9663676416 | bytes 1048576 | tf_op jit(solution)/shard_map/pallas_call | solution.py:440
  83.8 0.0 copy-start
  83.8 1.8 %copy.6 = f32[96,1024]{1,0:T(8,128)} copy(f32[96,1024]{1,0:T(8,128)} %get-tuple-element.8) | data formatting | bytes 786432
  85.6 0.0 copy-done
Async XLA Ops:
  83.8 1.8 %copy-start = (f32[1,128]{1,0:T(1,128)S(1)}, f32[1,128]{1,0:T(1,128)}, u32[]{:S(2)}) copy-start(f32[1,128]{1,0:T(1,128)} %get-tuple-element.5) | copy-start | bytes 1540

commit v2 on v1

v2 whole, which is shorter than its diff:
```python
import jax
import jax.numpy as jnp
from jax import lax
from jax.experimental import pallas as pl
from jax.experimental.pallas import tpu as pltpu
from jax.sharding import PartitionSpec as P

F32 = jnp.float32
BF16 = jnp.bfloat16
MESH = pl.DeviceIdType.MESH
LOG2E = 1.4426950408889634
NT = (((1,), (1,)), ((), ()))

BLOCK = 96
HALF = 48
DEPTH = 1024
N_Z = 8
ANCHORS = N_Z * BLOCK
KEYS = 32 * BLOCK
GROUP = 8 * BLOCK
CHUNKS = 4
WIDE = DEPTH // CHUNKS
TOKENS = 24576

A_POS = {0: 0, 7: 1, 1: 2, 6: 3, 2: 4, 5: 5, 3: 6, 4: 7}
K_ORDER = [
    (0, 0), (0, 3), (0, 1), (3, 0),
    (1, 0), (0, 2), (3, 3), (1, 3),
    (3, 1), (1, 1), (2, 0), (3, 2),
    (1, 2), (2, 3), (2, 1), (2, 2),
]
K_POS = {d: i for i, d in enumerate(K_ORDER)}
SHIFTS = (0, 96, 64, 32)
ARRIVALS = [
    ("A", 7, 0), ("A", 1, 0), ("K", 0, 3, 0), ("K", 0, 1, 0), ("K", 0, 3, 1), ("K", 0, 1, 1),
    ("A", 7, 1), ("A", 1, 1), ("K", 3, 0, 0), ("K", 1, 0, 0), ("K", 3, 0, 1), ("K", 1, 0, 1),
    ("A", 6, 0), ("A", 2, 0), ("K", 3, 1, 0), ("K", 1, 1, 0), ("K", 0, 2, 0), ("K", 0, 2, 1),
    ("K", 3, 3, 0), ("K", 1, 3, 0), ("A", 6, 1), ("A", 2, 1), ("K", 3, 1, 1), ("K", 1, 1, 1),
    ("K", 3, 3, 1), ("K", 1, 3, 1), ("A", 5, 0), ("A", 3, 0), ("K", 2, 0, 0), ("K", 2, 0, 1),
    ("A", 5, 1), ("A", 3, 1), ("K", 3, 2, 0), ("K", 1, 2, 0), ("K", 2, 1, 0), ("K", 3, 2, 1),
    ("K", 1, 2, 1), ("K", 2, 1, 1), ("K", 2, 3, 0), ("K", 2, 3, 1), ("A", 4, 0), ("A", 4, 1),
    ("K", 2, 2, 0), ("K", 2, 2, 1),
]
LABELS_AT = 13
LAG = 6


def key_row(core, dq, dp):
    q = K_POS[(dq, dp)]
    return (q // 4) * GROUP + core * (GROUP // 2) + (q % 4) * BLOCK


def key_slot(core, dq, dp):
    return core * 16 + K_POS[(dq, dp)]


class Semaphores:
    def __init__(self):
        self.numbers = {}

    def __call__(self, name):
        return self.numbers.setdefault(name, len(self.numbers))


N_SEM = 260


def kernel(emb, lab, grad, loss,
           own, au, ku, w, cm, g, uf, inv,
           var, al, kl, labc, klab,
           est, pst, cst, cto, cti, eto, eti, eio, iec, idc, kev, ke, kie,
           lz, lzi, lo, li, sb, rb, load, send, recv):
    row, z = lax.axis_index("row"), lax.axis_index("col")
    core, x, y = row % 2, (row // 2) % 4, row // 8
    number = Semaphores()
    pending = []

    def chip(dp, dq, other):
        px = (x + dp + core * (dq - dp) + 8) % 4
        py = (y + dq + core * (dp - dq) + 8) % 4
        pc = 1 - core if other else core
        return ((py * 4 + px) * 2 + pc, z)

    def up(dz):
        return (row, (z + dz + 8) % 8)

    def message(name, src, dst, to):
        i = number(name)
        return pltpu.make_async_remote_copy(
            src_ref=src, dst_ref=dst, send_sem=send.at[i], recv_sem=recv.at[i], device_id=to, device_id_type=MESH
        )

    def post(name, src, dst, to):
        copy = message(name, src, dst, to)
        copy.start()
        pending.append(copy)

    def arrived(name, dst):
        message(name, dst, dst, up(1)).wait_recv()

    def a_ref(dz, h):
        return au.at[pl.ds(A_POS[dz] * BLOCK + h * HALF, HALF), :]

    def k_ref(s, dq, dp, h):
        return ku.at[pl.ds(key_row(s, dq, dp) + h * HALF, HALF), :]

    peers = [(s, dq, dp) for s in (0, 1) for dq, dp in K_ORDER if (s, dq, dp) != (0, 0, 0)]

    barrier = pltpu.get_barrier_semaphore()
    for dz in range(1, N_Z):
        pl.semaphore_signal(barrier, inc=1, device_id=up(dz), device_id_type=MESH)
    for s, dq, dp in peers:
        pl.semaphore_signal(barrier, inc=1, device_id=chip(-dp, -dq, s), device_id_type=MESH)

    fetch = pltpu.make_async_copy(emb, own, load)
    fetch.start()
    own_label = jnp.zeros((1, 128), F32)
    al[0] = own_label
    al[0, :, 0:BLOCK] = lab[...].astype(F32)
    own_label = al[0]
    for p, shift in enumerate(SHIFTS):
        var[p] = pltpu.roll(own_label, shift, 1) if shift else own_label
    kl[0] = own_label
    est[...] = jnp.zeros_like(est)
    pst[...] = jnp.zeros_like(pst)
    cst[...] = jnp.zeros_like(cst)
    fetch.wait()
    wide = own[...].astype(F32)
    scale = lax.rsqrt(jnp.sum(wide * wide, axis=1, keepdims=True) + 1e-6)
    unit = wide * scale
    uf[...] = unit
    inv[...] = jnp.broadcast_to(scale, (BLOCK, 128))
    rounded = unit.astype(BF16)
    au[pl.ds(0, BLOCK), :] = rounded
    ku[pl.ds(0, BLOCK), :] = rounded
    pl.semaphore_wait(barrier, N_Z - 1 + len(peers))

    def ways_of(what):
        if what[0] == "A":
            _, dz, h = what
            if dz == 0:
                return [(0, 0, 1, 0, ("A", 7, h)), (0, 0, -1, 0, ("A", 1, h))]
            if dz in (7, 6) or (dz == 5 and h == 0):
                return [(0, 0, 1, 0, ("A", dz - 1, h))]
            if dz in (1, 2) or (dz == 3 and h == 1):
                return [(0, 0, -1, 0, ("A", dz + 1, h))]
            return []
        _, dq, dp, h = what
        ways = []
        if (dq, dp) == (0, 0):
            ways += [(1, 0, 0, 0, ("K", 0, 3, h)), (-1, 0, 0, 0, ("K", 0, 1, h))]
        elif (dq, dp, h) == (0, 3, 0):
            ways += [(1, 0, 0, 0, ("K", 0, 2, h))]
        elif (dq, dp, h) == (0, 1, 1):
            ways += [(-1, 0, 0, 0, ("K", 0, 2, h))]
        if dq == 0:
            ways += [(0, 1, 0, 0, ("K", 3, dp, h)), (0, -1, 0, 0, ("K", 1, dp, h))]
        elif dq == 3 and h == 0:
            ways += [(0, 1, 0, 0, ("K", 2, dp, h))]
        elif dq == 1 and h == 1:
            ways += [(0, -1, 0, 0, ("K", 2, dp, h))]
        return ways + [(0, 0, 0, 1, ("S", dq, dp, h))]

    def place(what):
        if what[0] == "A":
            return a_ref(what[1], what[2])
        return k_ref(1 if what[0] == "S" else 0, *what[1:])

    def forward(what, way):
        tp, tq, tz, ts, there = way
        post(there, place(what), place(there), up(tz) if tz else chip(tp, tq, bool(ts)))

    def hand_on(what):
        for way in ways_of(what):
            forward(what, way)

    for axes in ((0, 2), (1,), (3,)):
        for h in (0, 1):
            for what in (("K", 0, 0, h), ("A", 0, h)):
                for way in ways_of(what):
                    if any(way[i] for i in axes):
                        forward(what, way)
    for dz in range(1, N_Z):
        post(("L", 8 - dz), al.at[0], al.at[8 - dz], up(dz))
    for s, dq, dp in peers:
        post(("M", s, dq, dp), var.at[K_POS[(dq, dp)] % 4], kl.at[key_slot(s, dq, dp)], chip(-dp, -dq, s))

    lane = lax.broadcasted_iota(jnp.int32, (1, 128), 1)

    def columns(rows, out):
        turned = jnp.transpose(jnp.concatenate([rows, jnp.zeros((128 - N_Z, 128), F32)], axis=0))
        for dz, p in A_POS.items():
            out[pl.ds(p * BLOCK, BLOCK), :] = jnp.broadcast_to(turned[:BLOCK, dz : dz + 1], (BLOCK, 128))

    def lines(stat, out):
        for dz in range(N_Z):
            part = jnp.transpose(stat[pl.ds(A_POS[dz] * BLOCK, 128), :])
            out[dz : dz + 1, :] = jnp.sum(part, axis=0, keepdims=True)

    def exchange(name, out, into):
        for dz in (4, 3, 5, 2, 6, 1, 7):
            post((name, 8 - dz), out, into.at[8 - dz], up(dz))

    def gathered(name, out, into):
        total = out[...]
        for dz in range(1, N_Z):
            arrived((name, dz), into.at[dz])
            total = total + pltpu.roll(into[dz], dz, 0)
        return total

    def key_line(slots, out):
        for s in (0, 1):
            for q in range(4):
                m = [slots[s * 16 + q * 4 + p] for p in range(4)]
                base = q * GROUP + s * (GROUP // 2)
                for t, (cut, a, b) in enumerate(((96, 0, 1), (64, 1, 2), (32, 2, 3))):
                    line = jnp.where(lane < cut, m[a], m[b])
                    out[:, pl.ds(base + t * 128, 128)] = jnp.broadcast_to(line, (8, 128))

    def labels_ready():
        for dz in range(1, N_Z):
            arrived(("L", dz), al.at[dz])
        for s, dq, dp in peers:
            arrived(("M", s, dq, dp), kl.at[key_slot(s, dq, dp)])
        columns(jnp.concatenate([al[dz] for dz in range(N_Z)], axis=0), labc)
        key_line(kl, klab)

    def count(r0):
        for r in range(r0, r0 + 192, 32):
            label = labc[pl.ds(r, 32), :]
            total = jnp.zeros((32, 128), F32)
            for t in range(KEYS // 128):
                total = total + jnp.where(label == klab[0:1, t * 128 : (t + 1) * 128], 1.0, 0.0)
            cst[pl.ds(r, 32), :] = total
        if r0 == ANCHORS - 192:
            lines(cst, cto)
            exchange("C", cto, cti)

    def counts_ready():
        positives = gathered("C", cto, cti) - 1.0
        cto8 = jnp.where(lane < BLOCK, 2.0 / jnp.maximum(positives, 1.0), 0.0)
        columns(cto8, idc)
        eio[...] = positives[0:1] / jnp.maximum(positives[0:1], 1.0)

    def on_diagonal(rows):
        r = lax.broadcasted_iota(jnp.int32, (rows, 128), 0)
        c = lax.broadcasted_iota(jnp.int32, (rows, 128), 1)
        return (r == c) & (r < BLOCK)

    def score(r0, rows, c0, cols):
        at = pl.ds(r0, rows)
        acc = lax.dot_general(au[at, :], ku[pl.ds(c0, cols), :], NT, preferred_element_type=F32)
        label = labc[at, :]
        total = positive = None
        for t in range(cols // 128):
            here = pl.ds(c0 + t * 128, 128)
            s = acc[:, t * 128 : (t + 1) * 128]
            e = jnp.exp2(s * (10.0 * LOG2E) - 10.0 * LOG2E)
            same = label == klab[0:1, here]
            if r0 == 0 and c0 + t == 0:
                diagonal = on_diagonal(rows)
                e = jnp.where(diagonal, 0.0, e)
                same = same & ~diagonal
            w[at, here] = e
            ps = jnp.where(same, s, 0.0)
            if t == 0:
                total, positive = e, ps
            else:
                total, positive = total + e, positive + ps
        est[at, :] += total
        pst[at, :] += positive

    def need(r0, rows, c0, cols):
        wants = set()
        for dz, p in A_POS.items():
            if dz and p * BLOCK < r0 + rows and (p + 1) * BLOCK > r0:
                wants |= {("A", dz, 0), ("A", dz, 1)}
        for s in (0, 1):
            for dq, dp in K_ORDER:
                k0 = key_row(s, dq, dp)
                if k0 < c0 + cols and k0 + BLOCK > c0 and (s, dq, dp) != (0, 0, 0):
                    wants |= {("S" if s else "K", dq, dp, h) for h in (0, 1)}
        return wants

    work = [("count", r) for r in range(0, ANCHORS, 192)]
    for c in range(0, GROUP, 256):
        work.append((0, 480, c, 256))
    for c in range(0, GROUP, 256):
        work.append((0, 480, GROUP + c, 256))
    work.append(("done",))
    for c in range(0, 2 * GROUP, 256):
        work.append((480, 288, c, 256))
    for c in range(0, 2 * GROUP, 256):
        work.append((0, 768, 2 * GROUP + c, 256))

    seen = set()

    def receive(what):
        if what in seen:
            return
        seen.add(what)
        if what[0] == "A":
            arrived(what, a_ref(what[1], what[2]))
        else:
            arrived(what, k_ref(1 if what[0] == "S" else 0, *what[1:]))
        if what[0] != "S":
            hand_on(what)

    def can_run(wants):
        return all(v in seen for v in wants if v[0] != "S")

    def do(job):
        if job[0] == "count":
            count(job[1])
        elif job[0] == "done":
            counts_ready()
        else:
            for v in sorted(need(*job) - seen):
                receive(v)
            score(*job)

    def can_run(job, n):
        if isinstance(job[0], str):
            return True
        early = set(ARRIVALS[: max(n - LAG, 0)]) | {("K", 0, 0, 0), ("K", 0, 0, 1)}
        return all(v in seen or (v[0] == "S" and ("K",) + v[1:] in early) for v in need(*job))

    for n, what in enumerate(ARRIVALS):
        receive(what)
        if n == LABELS_AT:
            labels_ready()
        if n > LABELS_AT and work and n < len(ARRIVALS) - 1 and can_run(work[0], n):
            do(work.pop(0))
    for job in work:
        do(job)

    lines(est, eto)
    exchange("E", eto, eti)
    real = lane < BLOCK
    totals = jnp.where(real, gathered("E", eto, eti), 1.0)
    inverse_total = 1.0 / totals
    mine = inverse_total[0:1]
    for p, shift in enumerate(SHIFTS):
        kev[p] = pltpu.roll(mine, shift, 1) if shift else mine
    ke[0] = mine
    for s, dq, dp in reversed(peers):
        post(("V", s, dq, dp), kev.at[K_POS[(dq, dp)] % 4], ke.at[key_slot(s, dq, dp)], chip(-dp, -dq, s))
    columns(inverse_total, iec)
    share = jnp.sum(pst[0:ANCHORS, :] * idc[...], axis=0, keepdims=True) * -5.0
    tail = jnp.where(real, eio[...] * (jnp.log(totals[0:1]) + 10.0), 0.0)
    lz[...] = share + tail
    for dz in range(1, N_Z):
        post(("P", 8 - dz), lz, lzi.at[8 - dz], up(dz))
    for s, dq, dp in peers:
        arrived(("V", s, dq, dp), ke.at[key_slot(s, dq, dp)])
    key_line(ke, kie)

    def coupling(r0, rows):
        for r in range(r0, r0 + rows, 16):
            at = pl.ds(r, 16)
            ie, d2, label = iec[at, :], idc[at, :], labc[at, :]
            for c in range(0, KEYS, 128):
                here = pl.ds(c, 128)
                same = label == klab[0:1, here]
                if c == 0 and r < BLOCK:
                    i = lax.broadcasted_iota(jnp.int32, (16, 128), 0) + r
                    same = same & (i != lax.broadcasted_iota(jnp.int32, (16, 128), 1))
                v = w[at, here] * (ie + kie[0:1, here]) - jnp.where(same, d2, 0.0)
                cm[at, here] = v.astype(BF16)

    def product(j, r0, rows):
        at = pl.ds(r0, rows)
        g[j, at, :] = jnp.dot(cm[at, :], ku[:, j * WIDE : (j + 1) * WIDE], preferred_element_type=F32)

    def part(j, dz, first, n):
        return g[j, pl.ds(A_POS[dz] * BLOCK + first, n), :]

    def push(j, step):
        for way, sign in enumerate((1, -1)):
            dz = (sign * (4 - step)) % 8
            at, n = (way * HALF, HALF) if step == 0 else (0, BLOCK)
            value = part(j, dz, at, n)
            rows = pl.ds(at, n)
            if step == 1:
                half = pl.ds(way * HALF, HALF)
                arrived(("R", j, way, 0), rb.at[j, way, 0, half, :])
                pieces = [value[:HALF], value[HALF:]]
                pieces[way] = pieces[way] + rb[j, way, 0, half, :].astype(F32)
                sb[j, way, step, 0:HALF, :] = pieces[0].astype(BF16)
                sb[j, way, step, HALF:BLOCK, :] = pieces[1].astype(BF16)
            else:
                if step > 1:
                    arrived(("R", j, way, step - 1), rb.at[j, way, step - 1])
                    value = value + rb[j, way, step - 1].astype(F32)
                sb[j, way, step, rows, :] = value.astype(BF16)
            post(("R", j, way, step), sb.at[j, way, step, rows, :], rb.at[j, way, step, rows, :], up(sign))

    coupling(672, 96)
    for j in range(CHUNKS):
        product(j, 672, 96)
        push(j, 0)
    coupling(480, 192)
    for j in range(CHUNKS):
        product(j, 480, 192)
    coupling(288, 192)
    for j in range(CHUNKS):
        push(j, 1)
        product(j, 288, 192)
    coupling(96, 192)
    for j in range(CHUNKS):
        product(j, 96, 192)
    coupling(0, 96)
    for j in range(CHUNKS):
        push(j, 2)
        product(j, 0, 96)
    whole = lz[...]
    for dz in range(1, N_Z):
        arrived(("P", dz), lzi.at[dz])
        whole = whole + lzi[dz]
    lo[...] = whole
    for s, dq, dp in peers:
        post(("W", s, dq, dp), lo, li.at[key_slot(s, dq, dp)], chip(-dp, -dq, s))
    for j in range(CHUNKS):
        push(j, 3)

    every = lo[...]
    for s, dq, dp in peers:
        arrived(("W", s, dq, dp), li.at[key_slot(s, dq, dp)])
        every = every + li[key_slot(s, dq, dp)]
    loss[...] = jnp.broadcast_to(jnp.sum(every, axis=1, keepdims=True) * (1.0 / TOKENS), (1, 128))

    along = jnp.zeros((BLOCK, 1), F32)
    for j in range(CHUNKS):
        value = part(j, 0, 0, BLOCK)
        for way in (0, 1):
            arrived(("R", j, way, 3), rb.at[j, way, 3])
            value = value + rb[j, way, 3].astype(F32)
        value = value * 10.0
        g[j, pl.ds(0, BLOCK), :] = value
        along = along + jnp.sum(uf[:, j * WIDE : (j + 1) * WIDE] * value, axis=1, keepdims=True)
    scale = inv[:, 0:1]
    for j in range(CHUNKS):
        cut = slice(j * WIDE, (j + 1) * WIDE)
        grad[:, cut] = (g[j, pl.ds(0, BLOCK), :] - uf[:, cut] * along) * scale

    for copy in pending:
        copy.wait_send()
    assert len(number.numbers) <= N_SEM


def per_device(embeddings, labels):
    vmem = pl.BlockSpec(memory_space=pltpu.VMEM)
    line = labels.reshape(1, BLOCK)
    scratch = [
        ((BLOCK, DEPTH), BF16),
        ((ANCHORS, DEPTH), BF16),
        ((KEYS, DEPTH), BF16),
        ((ANCHORS, KEYS), F32),
        ((ANCHORS, KEYS), BF16),
        ((CHUNKS, ANCHORS, WIDE), F32),
        ((BLOCK, DEPTH), F32),
        ((BLOCK, 128), F32),
        ((4, 1, 128), F32),
        ((N_Z, 1, 128), F32),
        ((32, 1, 128), F32),
        ((ANCHORS, 128), F32),
        ((8, KEYS), F32),
        ((ANCHORS + 32, 128), F32),
        ((ANCHORS + 32, 128), F32),
        ((ANCHORS + 32, 128), F32),
        ((N_Z, 128), F32),
        ((N_Z, N_Z, 128), F32),
        ((N_Z, 128), F32),
        ((N_Z, N_Z, 128), F32),
        ((1, 128), F32),
        ((ANCHORS, 128), F32),
        ((ANCHORS, 128), F32),
        ((4, 1, 128), F32),
        ((32, 1, 128), F32),
        ((8, KEYS), F32),
        ((1, 128), F32),
        ((N_Z, 1, 128), F32),
        ((1, 128), F32),
        ((32, 1, 128), F32),
        ((CHUNKS, 2, 4, BLOCK, WIDE), BF16),
        ((CHUNKS, 2, 4, BLOCK, WIDE), BF16),
    ]
    grad, loss = pl.pallas_call(
        kernel,
        out_shape=(
            jax.ShapeDtypeStruct((BLOCK, DEPTH), F32),
            jax.ShapeDtypeStruct((1, 128), F32),
        ),
        in_specs=[pl.BlockSpec(memory_space=pl.ANY), vmem],
        out_specs=(vmem, vmem),
        scratch_shapes=[pltpu.VMEM(s, t) for s, t in scratch]
        + [pltpu.SemaphoreType.DMA, pltpu.SemaphoreType.DMA((N_SEM,)), pltpu.SemaphoreType.DMA((N_SEM,))],
        compiler_params=pltpu.CompilerParams(
            collective_id=0, has_side_effects=True, vmem_limit_bytes=60 * 2**20
        ),
        cost_estimate=pl.CostEstimate(flops=2 * 2 * ANCHORS * KEYS * DEPTH, bytes_accessed=2**20, transcendentals=0),
    )(embeddings, line)
    return grad, loss[0, 0]


def solution(mesh):
    placed = (P(("row", "col"), None), P(("row", "col")))
    return jax.shard_map(
        per_device,
        mesh=mesh,
        in_specs=placed,
        out_specs=(P(("row", "col"), None), P()),
        check_vma=False,
    )
```

time: 86.9 us -> 78.6 us (0.904)
  the two profiles are of different devices: /device:TPU:6 before, /device:TPU:1 now
where the time goes in v2:
time: 78.6 us; the launch traced here: 78.4 us
  Pallas kernels  74.9 us (95%)
  between operations  1.81 us (2%)
  local copies, waits for them, and re-layouts  1.77 us (2%)
    pallas_call x1, Pallas kernels, per_device(): pl.pallas_call(kernel, out_shape=(jax.ShapeDtypeStruct((BLOCK, DEPTH), F3...  74.9 us
    unnamed x3, local copies, waits for them, and re-layouts  1.77 us

profile of v2, /device:TPU:1, one launch (start us, length us, event | category | flops | bytes accessed | tf_op | source)
XLA Modules:
  0.0 78.4 jit_solution(14257137972294288791)
XLA Ops:
  0.6 74.9 %shard_map.41 = (f32[96,1024]{1,0:T(8,128)}, f32[1,128]{1,0:T(1,128)}) custom-call(bf16[96,1024]{1,0:T(8,128)(2,1)} %emb.1, s32[1,96]{1,0:T(1,128)} %bitcast.3), custom_call_target="tpu_custom_call" | custom-call | flops 9663676416 | bytes 1048576 | tf_op jit(solution)/shard_map/pallas_call | solution.py:488
  75.5 0.0 copy-start
  75.5 1.8 %copy.6 = f32[96,1024]{1,0:T(8,128)} copy(f32[96,1024]{1,0:T(8,128)} %get-tuple-element.8) | data formatting | bytes 786432
  77.3 0.0 copy-done
Async XLA Ops:
  75.5 1.8 %copy-start = (f32[1,128]{1,0:T(1,128)S(1)}, f32[1,128]{1,0:T(1,128)}, u32[]{:S(2)}) copy-start(f32[1,128]{1,0:T(1,128)} %get-tuple-element.5) | copy-start | bytes 1540

commit v3 on v2

--- a/solution.py
+++ b/solution.py
@@ -13,6 +13,8 @@
 
 BLOCK = 96
 HALF = 48
+PIECES = 3
+PIECE = BLOCK // PIECES
 DEPTH = 1024
 N_Z = 8
 ANCHORS = N_Z * BLOCK
@@ -32,17 +34,20 @@
 K_POS = {d: i for i, d in enumerate(K_ORDER)}
 SHIFTS = (0, 96, 64, 32)
 ARRIVALS = [
-    ("A", 7, 0), ("A", 1, 0), ("K", 0, 3, 0), ("K", 0, 1, 0), ("K", 0, 3, 1), ("K", 0, 1, 1),
-    ("A", 7, 1), ("A", 1, 1), ("K", 3, 0, 0), ("K", 1, 0, 0), ("K", 3, 0, 1), ("K", 1, 0, 1),
-    ("A", 6, 0), ("A", 2, 0), ("K", 3, 1, 0), ("K", 1, 1, 0), ("K", 0, 2, 0), ("K", 0, 2, 1),
-    ("K", 3, 3, 0), ("K", 1, 3, 0), ("A", 6, 1), ("A", 2, 1), ("K", 3, 1, 1), ("K", 1, 1, 1),
-    ("K", 3, 3, 1), ("K", 1, 3, 1), ("A", 5, 0), ("A", 3, 0), ("K", 2, 0, 0), ("K", 2, 0, 1),
-    ("A", 5, 1), ("A", 3, 1), ("K", 3, 2, 0), ("K", 1, 2, 0), ("K", 2, 1, 0), ("K", 3, 2, 1),
-    ("K", 1, 2, 1), ("K", 2, 1, 1), ("K", 2, 3, 0), ("K", 2, 3, 1), ("A", 4, 0), ("A", 4, 1),
-    ("K", 2, 2, 0), ("K", 2, 2, 1),
+    ("K", 0, 3, 0), ("K", 0, 1, 0), ("K", 0, 3, 1), ("K", 0, 1, 1), ("A", 7, 0), ("A", 1, 0),
+    ("K", 0, 3, 2), ("K", 0, 1, 2), ("K", 3, 0, 0), ("K", 1, 0, 0), ("A", 7, 1), ("A", 1, 1),
+    ("K", 3, 0, 1), ("K", 1, 0, 1), ("K", 3, 0, 2), ("K", 1, 0, 2), ("A", 7, 2), ("A", 1, 2),
+    ("K", 1, 3, 0), ("K", 0, 2, 0), ("K", 3, 3, 0), ("K", 1, 1, 0), ("K", 3, 1, 0), ("K", 1, 3, 1),
+    ("A", 6, 0), ("A", 2, 0), ("K", 3, 3, 1), ("K", 1, 1, 1), ("K", 0, 2, 1), ("K", 3, 1, 1),
+    ("A", 6, 1), ("A", 2, 1), ("K", 3, 3, 2), ("K", 1, 3, 2), ("K", 3, 1, 2), ("A", 6, 2),
+    ("A", 2, 2), ("K", 0, 2, 2), ("K", 1, 1, 2), ("K", 2, 0, 0), ("K", 2, 0, 1), ("K", 2, 0, 2),
+    ("K", 3, 2, 0), ("K", 1, 2, 0), ("K", 2, 3, 0), ("K", 2, 3, 1), ("A", 5, 0), ("A", 3, 0),
+    ("K", 2, 1, 0), ("K", 1, 2, 1), ("K", 3, 2, 1), ("K", 2, 3, 2), ("A", 5, 1), ("K", 2, 1, 1),
+    ("K", 1, 2, 2), ("K", 3, 2, 2), ("A", 3, 2), ("K", 2, 1, 2), ("A", 3, 1), ("K", 2, 2, 0),
+    ("K", 2, 2, 1), ("A", 5, 2), ("K", 2, 2, 2), ("A", 4, 2), ("A", 4, 0), ("A", 4, 1),
 ]
-LABELS_AT = 13
-LAG = 6
+LABELS_AT = 17
+LAG = 9
 
 
 def key_row(core, dq, dp):
@@ -68,7 +73,7 @@
 def kernel(emb, lab, grad, loss,
            own, au, ku, w, cm, g, uf, inv,
            var, al, kl, labc, klab,
-           est, pst, cst, cto, cti, eto, eti, eio, iec, idc, kev, ke, kie,
+           est, pst, cst, cto, cti, eto, eti, eio, iec, idc, cs, kso, ksi, kvo, kvi, kie,
            lz, lzi, lo, li, sb, rb, load, send, recv):
     row, z = lax.axis_index("row"), lax.axis_index("col")
     core, x, y = row % 2, (row // 2) % 4, row // 8
@@ -99,10 +104,10 @@
         message(name, dst, dst, up(1)).wait_recv()
 
     def a_ref(dz, h):
-        return au.at[pl.ds(A_POS[dz] * BLOCK + h * HALF, HALF), :]
+        return au.at[pl.ds(A_POS[dz] * BLOCK + h * PIECE, PIECE), :]
 
     def k_ref(s, dq, dp, h):
-        return ku.at[pl.ds(key_row(s, dq, dp) + h * HALF, HALF), :]
+        return ku.at[pl.ds(key_row(s, dq, dp) + h * PIECE, PIECE), :]
 
     peers = [(s, dq, dp) for s in (0, 1) for dq, dp in K_ORDER if (s, dq, dp) != (0, 0, 0)]
 
@@ -124,6 +129,7 @@
     est[...] = jnp.zeros_like(est)
     pst[...] = jnp.zeros_like(pst)
     cst[...] = jnp.zeros_like(cst)
+    cs[...] = jnp.zeros_like(cs)
     fetch.wait()
     wide = own[...].astype(F32)
     scale = lax.rsqrt(jnp.sum(wide * wide, axis=1, keepdims=True) + 1e-6)
@@ -135,29 +141,32 @@
     ku[pl.ds(0, BLOCK), :] = rounded
     pl.semaphore_wait(barrier, N_Z - 1 + len(peers))
 
+    def upward(dp, h):
+        return h == 0 or (h == 1 and dp < 2)
+
     def ways_of(what):
         if what[0] == "A":
             _, dz, h = what
             if dz == 0:
                 return [(0, 0, 1, 0, ("A", 7, h)), (0, 0, -1, 0, ("A", 1, h))]
-            if dz in (7, 6) or (dz == 5 and h == 0):
+            if dz in (7, 6) or (dz == 5 and upward(0, h)):
                 return [(0, 0, 1, 0, ("A", dz - 1, h))]
-            if dz in (1, 2) or (dz == 3 and h == 1):
+            if dz in (1, 2) or (dz == 3 and not upward(0, h)):
                 return [(0, 0, -1, 0, ("A", dz + 1, h))]
             return []
         _, dq, dp, h = what
         ways = []
         if (dq, dp) == (0, 0):
             ways += [(1, 0, 0, 0, ("K", 0, 3, h)), (-1, 0, 0, 0, ("K", 0, 1, h))]
-        elif (dq, dp, h) == (0, 3, 0):
+        elif (dq, dp) == (0, 3) and upward(2, h):
             ways += [(1, 0, 0, 0, ("K", 0, 2, h))]
-        elif (dq, dp, h) == (0, 1, 1):
+        elif (dq, dp) == (0, 1) and not upward(2, h):
             ways += [(-1, 0, 0, 0, ("K", 0, 2, h))]
         if dq == 0:
             ways += [(0, 1, 0, 0, ("K", 3, dp, h)), (0, -1, 0, 0, ("K", 1, dp, h))]
-        elif dq == 3 and h == 0:
+        elif dq == 3 and upward(dp, h):
             ways += [(0, 1, 0, 0, ("K", 2, dp, h))]
-        elif dq == 1 and h == 1:
+        elif dq == 1 and not upward(dp, h):
             ways += [(0, -1, 0, 0, ("K", 2, dp, h))]
         return ways + [(0, 0, 0, 1, ("S", dq, dp, h))]
 
@@ -175,7 +184,7 @@
             forward(what, way)
 
     for axes in ((0, 2), (1,), (3,)):
-        for h in (0, 1):
+        for h in range(PIECES):
             for what in (("K", 0, 0, h), ("A", 0, h)):
                 for way in ways_of(what):
                     if any(way[i] for i in axes):
@@ -208,10 +217,10 @@
             total = total + pltpu.roll(into[dz], dz, 0)
         return total
 
-    def key_line(slots, out):
+    def key_line(line_of, out):
         for s in (0, 1):
             for q in range(4):
-                m = [slots[s * 16 + q * 4 + p] for p in range(4)]
+                m = [line_of(s, q * 4 + p) for p in range(4)]
                 base = q * GROUP + s * (GROUP // 2)
                 for t, (cut, a, b) in enumerate(((96, 0, 1), (64, 1, 2), (32, 2, 3))):
                     line = jnp.where(lane < cut, m[a], m[b])
@@ -223,7 +232,7 @@
         for s, dq, dp in peers:
             arrived(("M", s, dq, dp), kl.at[key_slot(s, dq, dp)])
         columns(jnp.concatenate([al[dz] for dz in range(N_Z)], axis=0), labc)
-        key_line(kl, klab)
+        key_line(lambda s, q: kl[s * 16 + q], klab)
 
     def count(r0):
         for r in range(r0, r0 + 192, 32):
@@ -262,6 +271,7 @@
                 e = jnp.where(diagonal, 0.0, e)
                 same = same & ~diagonal
             w[at, here] = e
+            cs[:, here] += jnp.sum(e.reshape(rows // 8, 8, 128), axis=0)
             ps = jnp.where(same, s, 0.0)
             if t == 0:
                 total, positive = e, ps
@@ -274,12 +284,12 @@
         wants = set()
         for dz, p in A_POS.items():
             if dz and p * BLOCK < r0 + rows and (p + 1) * BLOCK > r0:
-                wants |= {("A", dz, 0), ("A", dz, 1)}
+                wants |= {("A", dz, h) for h in range(PIECES)}
         for s in (0, 1):
             for dq, dp in K_ORDER:
                 k0 = key_row(s, dq, dp)
                 if k0 < c0 + cols and k0 + BLOCK > c0 and (s, dq, dp) != (0, 0, 0):
-                    wants |= {("S" if s else "K", dq, dp, h) for h in (0, 1)}
+                    wants |= {("S" if s else "K", dq, dp, h) for h in range(PIECES)}
         return wants
 
     work = [("count", r) for r in range(0, ANCHORS, 192)]
@@ -322,7 +332,7 @@
     def can_run(job, n):
         if isinstance(job[0], str):
             return True
-        early = set(ARRIVALS[: max(n - LAG, 0)]) | {("K", 0, 0, 0), ("K", 0, 0, 1)}
+        early = set(ARRIVALS[: max(n - LAG, 0)]) | {("K", 0, 0, h) for h in range(PIECES)}
         return all(v in seen or (v[0] == "S" and ("K",) + v[1:] in early) for v in need(*job))
 
     for n, what in enumerate(ARRIVALS):
@@ -334,26 +344,64 @@
     for job in work:
         do(job)
 
+    tiles = [jnp.sum(cs[:, t * 128 : (t + 1) * 128], axis=0, keepdims=True) for t in range(KEYS // 128)]
+    for s in (0, 1):
+        for dq, dp in K_ORDER:
+            t, off = divmod(key_row(s, dq, dp), 128)
+            line = tiles[t]
+            if off:
+                line = pltpu.roll(line, 128 - off, 1)
+                if off + BLOCK > 128:
+                    line = jnp.where(lane < 128 - off, line, pltpu.roll(tiles[t + 1], 128 - off, 1))
+            r = s * 16 + dq * 4 + dp
+            kso[r : r + 1, :] = line
+    post(("X",), kso, ksi, chip(0, 0, True))
     lines(est, eto)
     exchange("E", eto, eti)
+    arrived(("X",), ksi)
+    both = [kso[0:16, :] + ksi[16:32, :], kso[16:32, :] + ksi[0:16, :]]
+    kvo[0:16, :] = both[0].astype(BF16)
+    kvo[16:32, :] = both[1].astype(BF16)
+    plane = [(dq, dp) for dq, dp in reversed(K_ORDER) if (dq, dp) != (0, 0)]
+    for dq, dp in plane:
+        post(("V", dq, dp), kvo, kvi.at[dq * 4 + dp], chip(-dp, -dq, False))
     real = lane < BLOCK
     totals = jnp.where(real, gathered("E", eto, eti), 1.0)
     inverse_total = 1.0 / totals
-    mine = inverse_total[0:1]
-    for p, shift in enumerate(SHIFTS):
-        kev[p] = pltpu.roll(mine, shift, 1) if shift else mine
-    ke[0] = mine
-    for s, dq, dp in reversed(peers):
-        post(("V", s, dq, dp), kev.at[K_POS[(dq, dp)] % 4], ke.at[key_slot(s, dq, dp)], chip(-dp, -dq, s))
     columns(inverse_total, iec)
     share = jnp.sum(pst[0:ANCHORS, :] * idc[...], axis=0, keepdims=True) * -5.0
     tail = jnp.where(real, eio[...] * (jnp.log(totals[0:1]) + 10.0), 0.0)
     lz[...] = share + tail
     for dz in range(1, N_Z):
         post(("P", 8 - dz), lz, lzi.at[8 - dz], up(dz))
-    for s, dq, dp in peers:
-        arrived(("V", s, dq, dp), ke.at[key_slot(s, dq, dp)])
-    key_line(ke, kie)
+    for dq, dp in plane:
+        arrived(("V", dq, dp), kvi.at[dq * 4 + dp])
+    within = lax.broadcasted_iota(jnp.int32, (16, 128), 0) % 4
+    turned = []
+    for s in (0, 1):
+        total = both[s]
+        for b in range(4):
+            by_q = None
+            for a in range(4):
+                dq, dp = (b, a) if s else (a, b)
+                if (dq, dp) == (0, 0):
+                    continue
+                value = kvi[dq * 4 + dp, s * 16 : s * 16 + 16, :].astype(F32)
+                if a:
+                    value = pltpu.roll(value, 4 * a, 0)
+                by_q = value if by_q is None else by_q + value
+            if b:
+                by_q = jnp.where(within < b, pltpu.roll(by_q, 12 + b, 0), pltpu.roll(by_q, b, 0))
+            total = total + by_q
+        inverse = 1.0 / total
+        turned.append([pltpu.roll(inverse, shift, 1) if shift else inverse for shift in SHIFTS])
+
+    def inverse_line(s, q):
+        dq, dp = K_ORDER[q]
+        r = dq * 4 + dp
+        return turned[s][q % 4][r : r + 1, :]
+
+    key_line(inverse_line, kie)
 
     def coupling(r0, rows):
         for r in range(r0, r0 + rows, 16):
@@ -475,8 +523,11 @@
         ((1, 128), F32),
         ((ANCHORS, 128), F32),
         ((ANCHORS, 128), F32),
-        ((4, 1, 128), F32),
-        ((32, 1, 128), F32),
+        ((8, KEYS), F32),
+        ((32, 128), F32),
+        ((32, 128), F32),
+        ((32, 128), BF16),
+        ((16, 32, 128), BF16),
         ((8, KEYS), F32),
         ((1, 128), F32),
         ((N_Z, 1, 128), F32),
@@ -491,12 +542,12 @@
             jax.ShapeDtypeStruct((BLOCK, DEPTH), F32),
             jax.ShapeDtypeStruct((1, 128), F32),
         ),
-        in_specs=[pl.BlockSpec(memory_space=pl.ANY), vmem],
+        in_specs=[pl.BlockSpec(memory_space=pltpu.HBM), vmem],
         out_specs=(vmem, vmem),
         scratch_shapes=[pltpu.VMEM(s, t) for s, t in scratch]
         + [pltpu.SemaphoreType.DMA, pltpu.SemaphoreType.DMA((N_SEM,)), pltpu.SemaphoreType.DMA((N_SEM,))],
         compiler_params=pltpu.CompilerParams(
-            collective_id=0, has_side_effects=True, vmem_limit_bytes=60 * 2**20
+            collective_id=0, has_side_effects=True, vmem_limit_bytes=44 * 2**20
         ),
         cost_estimate=pl.CostEstimate(flops=2 * 2 * ANCHORS * KEYS * DEPTH, bytes_accessed=2**20, transcendentals=0),
     )(embeddings, line)

time: 78.6 us -> 73.7 us (0.938)
  Pallas kernels: 74.9 us -> 69.4 us
    pallas_call x1, Pallas kernels: 74.9 us -> 69.4 us  [per_device(): pl.pallas_call(kernel, out_shape=(jax.ShapeDtypeStruct((BLOCK, DEPTH), F3...]
    unnamed x3 -> x5, local copies, waits for them, and re-layouts: 1.77 us -> 2.32 us
where the time goes in v3:
time: 73.7 us; the launch traced here: 73.6 us
  Pallas kernels  69.4 us (94%)
  local copies, waits for them, and re-layouts  2.32 us (3%)
  between operations  1.81 us (2%)
    pallas_call x1, Pallas kernels, per_device(): pl.pallas_call(kernel, out_shape=(jax.ShapeDtypeStruct((BLOCK, DEPTH), F3...  69.4 us
    unnamed x5, local copies, waits for them, and re-layouts  2.32 us

profile of v3, /device:TPU:1, one launch (start us, length us, event | category | flops | bytes accessed | tf_op | source)
XLA Modules:
  0.0 73.6 jit_solution(16287186594991033580)
XLA Ops:
  0.6 0.0 copy-start.1
  0.6 0.6 copy-done.1
  1.3 0.0 copy-start
  1.3 0.9 %copy-done = bf16[96,1024]{1,0:T(8,128)(2,1)S(1)} copy-done((bf16[96,1024]{1,0:T(8,128)(2,1)S(1)}, bf16[96,1024]{1,0:T(8,128)(2,1)}, u32[]{:S(2)}) %copy-start) | copy-done | bytes 196632
  2.2 69.4 %shard_map.41 = (f32[96,1024]{1,0:T(8,128)S(1)}, f32[1,128]{1,0:T(1,128)S(1)}) custom-call(bf16[96,1024]{1,0:T(8,128)(2,1)S(1)} %copy-done, s32[1,96]{1,0:T(1,128)S(1)} %bitcast.3), custom_call_target="tpu_custom_call" | custom-call | flops 9663676416 | bytes 1048576 | tf_op jit(solution)/shard_map/pallas_call | solution.py:539
  71.7 0.7 %copy.6 = f32[96,1024]{1,0:T(8,128)} copy(f32[96,1024]{1,0:T(8,128)S(1)} %get-tuple-element.8) | data formatting | bytes 786432
Async XLA Ops:
  0.6 0.7 copy-start.1
  1.3 0.9 %copy-start = (bf16[96,1024]{1,0:T(8,128)(2,1)S(1)}, bf16[96,1024]{1,0:T(8,128)(2,1)}, u32[]{:S(2)}) copy-start(bf16[96,1024]{1,0:T(8,128)(2,1)} %emb.1) | copy-start | bytes 589828

commit v4 on v3

--- a/solution.py
+++ b/solution.py
@@ -27,9 +27,9 @@
 A_POS = {0: 0, 7: 1, 1: 2, 6: 3, 2: 4, 5: 5, 3: 6, 4: 7}
 K_ORDER = [
     (0, 0), (0, 3), (0, 1), (3, 0),
-    (1, 0), (0, 2), (3, 3), (1, 3),
-    (3, 1), (1, 1), (2, 0), (3, 2),
-    (1, 2), (2, 3), (2, 1), (2, 2),
+    (1, 0), (3, 3), (1, 3), (3, 1),
+    (0, 2), (1, 1), (2, 0), (2, 3),
+    (1, 2), (3, 2), (2, 1), (2, 2),
 ]
 K_POS = {d: i for i, d in enumerate(K_ORDER)}
 SHIFTS = (0, 96, 64, 32)
@@ -42,12 +42,14 @@
     ("A", 6, 1), ("A", 2, 1), ("K", 3, 3, 2), ("K", 1, 3, 2), ("K", 3, 1, 2), ("A", 6, 2),
     ("A", 2, 2), ("K", 0, 2, 2), ("K", 1, 1, 2), ("K", 2, 0, 0), ("K", 2, 0, 1), ("K", 2, 0, 2),
     ("K", 3, 2, 0), ("K", 1, 2, 0), ("K", 2, 3, 0), ("K", 2, 3, 1), ("A", 5, 0), ("A", 3, 0),
-    ("K", 2, 1, 0), ("K", 1, 2, 1), ("K", 3, 2, 1), ("K", 2, 3, 2), ("A", 5, 1), ("K", 2, 1, 1),
-    ("K", 1, 2, 2), ("K", 3, 2, 2), ("A", 3, 2), ("K", 2, 1, 2), ("A", 3, 1), ("K", 2, 2, 0),
-    ("K", 2, 2, 1), ("A", 5, 2), ("K", 2, 2, 2), ("A", 4, 2), ("A", 4, 0), ("A", 4, 1),
+    ("K", 2, 1, 0), ("K", 1, 2, 1), ("K", 3, 2, 1), ("K", 2, 3, 2), ("A", 5, 1), ("A", 3, 1),
+    ("K", 2, 1, 1), ("K", 1, 2, 2), ("K", 3, 2, 2), ("A", 3, 2), ("A", 5, 2), ("K", 2, 1, 2),
+    ("K", 2, 2, 0), ("K", 2, 2, 1), ("K", 2, 2, 2), ("A", 4, 2), ("A", 4, 0), ("A", 4, 1),
 ]
 LABELS_AT = 17
-LAG = 9
+JOBS_AFTER = {
+    17: (0,), 18: (1, 2), 21: (3, 4), 25: (5,), 26: (6,), 36: (7, 8, 9, 11), 41: (12, 13), 44: (10,), 58: (14,), 59: (15, 16, 17), 60: (18, 19, 20), 61: (21, 22), 62: (23, 24),
+}
 
 
 def key_row(core, dq, dp):
@@ -71,7 +73,7 @@
 
 
 def kernel(emb, lab, grad, loss,
-           own, au, ku, w, cm, g, uf, inv,
+           own, own_line, au, ku, w, cm, g, uf, inv,
            var, al, kl, labc, klab,
            est, pst, cst, cto, cti, eto, eti, eio, iec, idc, cs, kso, ksi, kvo, kvi, kie,
            lz, lzi, lo, li, sb, rb, load, send, recv):
@@ -117,19 +119,21 @@
     for s, dq, dp in peers:
         pl.semaphore_signal(barrier, inc=1, device_id=chip(-dp, -dq, s), device_id_type=MESH)
 
-    fetch = pltpu.make_async_copy(emb, own, load)
+    fetch = pltpu.make_async_copy(emb, own, load.at[0])
     fetch.start()
-    own_label = jnp.zeros((1, 128), F32)
-    al[0] = own_label
-    al[0, :, 0:BLOCK] = lab[...].astype(F32)
+    fetch_line = pltpu.make_async_copy(lab, own_line, load.at[1])
+    fetch_line.start()
+    est[...] = jnp.zeros_like(est)
+    pst[...] = jnp.zeros_like(pst)
+    cst[...] = jnp.zeros_like(cst)
+    cs[...] = jnp.zeros_like(cs)
+    al[0] = jnp.zeros((1, 128), F32)
+    fetch_line.wait()
+    al[0, :, 0:BLOCK] = own_line[...].astype(F32)
     own_label = al[0]
     for p, shift in enumerate(SHIFTS):
         var[p] = pltpu.roll(own_label, shift, 1) if shift else own_label
     kl[0] = own_label
-    est[...] = jnp.zeros_like(est)
-    pst[...] = jnp.zeros_like(pst)
-    cst[...] = jnp.zeros_like(cst)
-    cs[...] = jnp.zeros_like(cs)
     fetch.wait()
     wide = own[...].astype(F32)
     scale = lax.rsqrt(jnp.sum(wide * wide, axis=1, keepdims=True) + 1e-6)
@@ -293,15 +297,19 @@
         return wants
 
     work = [("count", r) for r in range(0, ANCHORS, 192)]
-    for c in range(0, GROUP, 256):
-        work.append((0, 480, c, 256))
-    for c in range(0, GROUP, 256):
-        work.append((0, 480, GROUP + c, 256))
-    work.append(("done",))
-    for c in range(0, 2 * GROUP, 256):
-        work.append((480, 288, c, 256))
-    for c in range(0, 2 * GROUP, 256):
-        work.append((0, 768, 2 * GROUP + c, 256))
+    for r0, rows, c0, c1, wide in (
+        (0, 288, 0, GROUP, 256),
+        (288, 192, 0, GROUP, 256),
+        (0, 480, GROUP, 2 * GROUP, 256),
+        (480, 192, 0, 2 * GROUP, 256),
+        (0, 672, 2 * GROUP, 3 * GROUP, 256),
+        (0, 672, 3 * GROUP, 3 * GROUP + 512, 256),
+        (672, 96, 0, 3 * GROUP, GROUP),
+        (0, 672, 3 * GROUP + 512, 4 * GROUP, 256),
+        (672, 96, 3 * GROUP, 4 * GROUP, GROUP),
+    ):
+        work += [(r0, rows, c, wide) for c in range(c0, c1, wide)]
+    work.insert(10, ("done",))
 
     seen = set()
 
@@ -329,20 +337,16 @@
                 receive(v)
             score(*job)
 
-    def can_run(job, n):
-        if isinstance(job[0], str):
-            return True
-        early = set(ARRIVALS[: max(n - LAG, 0)]) | {("K", 0, 0, h) for h in range(PIECES)}
-        return all(v in seen or (v[0] == "S" and ("K",) + v[1:] in early) for v in need(*job))
-
+    left = list(range(len(work)))
     for n, what in enumerate(ARRIVALS):
         receive(what)
         if n == LABELS_AT:
             labels_ready()
-        if n > LABELS_AT and work and n < len(ARRIVALS) - 1 and can_run(work[0], n):
-            do(work.pop(0))
-    for job in work:
-        do(job)
+        for i in JOBS_AFTER.get(n, ()):
+            do(work[i])
+            left.remove(i)
+    for i in left:
+        do(work[i])
 
     tiles = [jnp.sum(cs[:, t * 128 : (t + 1) * 128], axis=0, keepdims=True) for t in range(KEYS // 128)]
     for s in (0, 1):
@@ -501,6 +505,7 @@
     line = labels.reshape(1, BLOCK)
     scratch = [
         ((BLOCK, DEPTH), BF16),
+        ((1, BLOCK), jnp.int32),
         ((ANCHORS, DEPTH), BF16),
         ((KEYS, DEPTH), BF16),
         ((ANCHORS, KEYS), F32),
@@ -539,15 +544,15 @@
     grad, loss = pl.pallas_call(
         kernel,
         out_shape=(
-            jax.ShapeDtypeStruct((BLOCK, DEPTH), F32),
+            pltpu.VMEM((BLOCK, DEPTH), F32),
             jax.ShapeDtypeStruct((1, 128), F32),
         ),
-        in_specs=[pl.BlockSpec(memory_space=pltpu.HBM), vmem],
+        in_specs=[pl.BlockSpec(memory_space=pl.ANY)] * 2,
         out_specs=(vmem, vmem),
         scratch_shapes=[pltpu.VMEM(s, t) for s, t in scratch]
-        + [pltpu.SemaphoreType.DMA, pltpu.SemaphoreType.DMA((N_SEM,)), pltpu.SemaphoreType.DMA((N_SEM,))],
+        + [pltpu.SemaphoreType.DMA((2,)), pltpu.SemaphoreType.DMA((N_SEM,)), pltpu.SemaphoreType.DMA((N_SEM,))],
         compiler_params=pltpu.CompilerParams(
-            collective_id=0, has_side_effects=True, vmem_limit_bytes=44 * 2**20
+            collective_id=0, has_side_effects=True, vmem_limit_bytes=60 * 2**20
         ),
         cost_estimate=pl.CostEstimate(flops=2 * 2 * ANCHORS * KEYS * DEPTH, bytes_accessed=2**20, transcendentals=0),
     )(embeddings, line)

time: 73.7 us -> 72.1 us (0.978)
  local copies, waits for them, and re-layouts: 2.32 us -> 0.75 us
    unnamed x5 -> x3, local copies, waits for them, and re-layouts: 2.32 us -> 0.75 us
where the time goes in v4:
time: 72.1 us; the launch traced here: 72 us
  Pallas kernels  69.5 us (96%)
  between operations  1.81 us (3%)
  local copies, waits for them, and re-layouts  0.75 us (1%)
    pallas_call x1, Pallas kernels, per_device(): pl.pallas_call(kernel, out_shape=(pltpu.VMEM((BLOCK, DEPTH), F32), jax.Sh...  69.5 us

profile of v4, /device:TPU:1, one launch (start us, length us, event | category | flops | bytes accessed | tf_op | source)
XLA Modules:
  0.0 72.0 jit_solution(4329444721572340765)
XLA Ops:
  0.6 69.5 %shard_map.41 = (f32[96,1024]{1,0:T(8,128)S(1)}, f32[1,128]{1,0:T(1,128)}) custom-call(bf16[96,1024]{1,0:T(8,128)(2,1)} %emb.1, s32[1,96]{1,0:T(1,128)} %bitcast.3), custom_call_target="tpu_custom_call" | custom-call | flops 9663676416 | bytes 1048576 | tf_op jit(solution)/shard_map/pallas_call | solution.py:544
  70.1 0.0 copy-start
  70.1 0.7 %copy.6 = f32[96,1024]{1,0:T(8,128)} copy(f32[96,1024]{1,0:T(8,128)S(1)} %get-tuple-element.6) | data formatting | bytes 786432
  70.9 0.0 copy-done
Async XLA Ops:
  70.1 0.8 %copy-start = (f32[1,128]{1,0:T(1,128)S(1)}, f32[1,128]{1,0:T(1,128)}, u32[]{:S(2)}) copy-start(f32[1,128]{1,0:T(1,128)} %get-tuple-element.5) | copy-start | bytes 1540

commit v5 on v4

--- a/solution.py
+++ b/solution.py
@@ -46,9 +46,9 @@
     ("K", 2, 1, 1), ("K", 1, 2, 2), ("K", 3, 2, 2), ("A", 3, 2), ("A", 5, 2), ("K", 2, 1, 2),
     ("K", 2, 2, 0), ("K", 2, 2, 1), ("K", 2, 2, 2), ("A", 4, 2), ("A", 4, 0), ("A", 4, 1),
 ]
-LABELS_AT = 17
 JOBS_AFTER = {
-    17: (0,), 18: (1, 2), 21: (3, 4), 25: (5,), 26: (6,), 36: (7, 8, 9, 11), 41: (12, 13), 44: (10,), 58: (14,), 59: (15, 16, 17), 60: (18, 19, 20), 61: (21, 22), 62: (23, 24),
+    17: (0, 1), 21: (2,), 36: (3, 4, 5), 39: (6,), 41: (7, 8), 59: (9, 10, 11), 60: (12, 13, 14, 15), 61: (16, 17),
+
 }
 
 
@@ -69,12 +69,12 @@
         return self.numbers.setdefault(name, len(self.numbers))
 
 
-N_SEM = 260
+N_SEM = 340
 
 
 def kernel(emb, lab, grad, loss,
            own, own_line, au, ku, w, cm, g, uf, inv,
-           var, al, kl, labc, klab,
+           al, kl, labc, klab,
            est, pst, cst, cto, cti, eto, eti, eio, iec, idc, cs, kso, ksi, kvo, kvi, kie,
            lz, lzi, lo, li, sb, rb, load, send, recv):
     row, z = lax.axis_index("row"), lax.axis_index("col")
@@ -113,27 +113,22 @@
 
     peers = [(s, dq, dp) for s in (0, 1) for dq, dp in K_ORDER if (s, dq, dp) != (0, 0, 0)]
 
+    near = [up(1), up(-1), chip(1, 0, 0), chip(-1, 0, 0), chip(0, 1, 0), chip(0, -1, 0), chip(0, 0, 1)]
     barrier = pltpu.get_barrier_semaphore()
-    for dz in range(1, N_Z):
-        pl.semaphore_signal(barrier, inc=1, device_id=up(dz), device_id_type=MESH)
-    for s, dq, dp in peers:
-        pl.semaphore_signal(barrier, inc=1, device_id=chip(-dp, -dq, s), device_id_type=MESH)
+    for other in near:
+        pl.semaphore_signal(barrier, inc=1, device_id=other, device_id_type=MESH)
 
     fetch = pltpu.make_async_copy(emb, own, load.at[0])
     fetch.start()
     fetch_line = pltpu.make_async_copy(lab, own_line, load.at[1])
     fetch_line.start()
     est[...] = jnp.zeros_like(est)
-    pst[...] = jnp.zeros_like(pst)
     cst[...] = jnp.zeros_like(cst)
     cs[...] = jnp.zeros_like(cs)
     al[0] = jnp.zeros((1, 128), F32)
     fetch_line.wait()
     al[0, :, 0:BLOCK] = own_line[...].astype(F32)
-    own_label = al[0]
-    for p, shift in enumerate(SHIFTS):
-        var[p] = pltpu.roll(own_label, shift, 1) if shift else own_label
-    kl[0] = own_label
+    kl[0] = al[0]
     fetch.wait()
     wide = own[...].astype(F32)
     scale = lax.rsqrt(jnp.sum(wide * wide, axis=1, keepdims=True) + 1e-6)
@@ -143,7 +138,7 @@
     rounded = unit.astype(BF16)
     au[pl.ds(0, BLOCK), :] = rounded
     ku[pl.ds(0, BLOCK), :] = rounded
-    pl.semaphore_wait(barrier, N_Z - 1 + len(peers))
+    pl.semaphore_wait(barrier, len(near))
 
     def upward(dp, h):
         return h == 0 or (h == 1 and dp < 2)
@@ -179,9 +174,17 @@
             return a_ref(what[1], what[2])
         return k_ref(1 if what[0] == "S" else 0, *what[1:])
 
+    def line_place(what):
+        if what[0] == "A":
+            return al.at[what[1]]
+        return kl.at[key_slot(1 if what[0] == "S" else 0, what[1], what[2])]
+
     def forward(what, way):
         tp, tq, tz, ts, there = way
-        post(there, place(what), place(there), up(tz) if tz else chip(tp, tq, bool(ts)))
+        to = up(tz) if tz else chip(tp, tq, bool(ts))
+        if what[-1] == 0:
+            post(("L",) + there, line_place(what), line_place(there), to)
+        post(there, place(what), place(there), to)
 
     def hand_on(what):
         for way in ways_of(what):
@@ -193,11 +196,6 @@
                 for way in ways_of(what):
                     if any(way[i] for i in axes):
                         forward(what, way)
-    for dz in range(1, N_Z):
-        post(("L", 8 - dz), al.at[0], al.at[8 - dz], up(dz))
-    for s, dq, dp in peers:
-        post(("M", s, dq, dp), var.at[K_POS[(dq, dp)] % 4], kl.at[key_slot(s, dq, dp)], chip(-dp, -dq, s))
-
     lane = lax.broadcasted_iota(jnp.int32, (1, 128), 1)
 
     def columns(rows, out):
@@ -231,29 +229,28 @@
                     out[:, pl.ds(base + t * 128, 128)] = jnp.broadcast_to(line, (8, 128))
 
     def labels_ready():
-        for dz in range(1, N_Z):
-            arrived(("L", dz), al.at[dz])
-        for s, dq, dp in peers:
-            arrived(("M", s, dq, dp), kl.at[key_slot(s, dq, dp)])
         columns(jnp.concatenate([al[dz] for dz in range(N_Z)], axis=0), labc)
-        key_line(lambda s, q: kl[s * 16 + q], klab)
-
-    def count(r0):
-        for r in range(r0, r0 + 192, 32):
+
+        def label_line(s, q):
+            line = kl[s * 16 + q]
+            return pltpu.roll(line, SHIFTS[q % 4], 1) if q % 4 else line
+
+        key_line(label_line, klab)
+
+    def count():
+        for r in range(0, ANCHORS, 32):
             label = labc[pl.ds(r, 32), :]
             total = jnp.zeros((32, 128), F32)
             for t in range(KEYS // 128):
                 total = total + jnp.where(label == klab[0:1, t * 128 : (t + 1) * 128], 1.0, 0.0)
             cst[pl.ds(r, 32), :] = total
-        if r0 == ANCHORS - 192:
-            lines(cst, cto)
-            exchange("C", cto, cti)
+        lines(cst, cto)
+        exchange("C", cto, cti)
 
     def counts_ready():
-        positives = gathered("C", cto, cti) - 1.0
-        cto8 = jnp.where(lane < BLOCK, 2.0 / jnp.maximum(positives, 1.0), 0.0)
-        columns(cto8, idc)
-        eio[...] = positives[0:1] / jnp.maximum(positives[0:1], 1.0)
+        others = gathered("C", cto, cti) - 1.0
+        columns(jnp.where(lane < BLOCK, 2.0 / jnp.maximum(others, 1.0), 0.0), idc)
+        eio[...] = others[0:1] / jnp.maximum(others[0:1], 1.0)
 
     def on_diagonal(rows):
         r = lax.broadcasted_iota(jnp.int32, (rows, 128), 0)
@@ -263,26 +260,31 @@
     def score(r0, rows, c0, cols):
         at = pl.ds(r0, rows)
         acc = lax.dot_general(au[at, :], ku[pl.ds(c0, cols), :], NT, preferred_element_type=F32)
-        label = labc[at, :]
-        total = positive = None
+        total = None
         for t in range(cols // 128):
             here = pl.ds(c0 + t * 128, 128)
             s = acc[:, t * 128 : (t + 1) * 128]
-            e = jnp.exp2(s * (10.0 * LOG2E) - 10.0 * LOG2E)
-            same = label == klab[0:1, here]
+            w[at, here] = s
+            e = jnp.exp2(s * (10.0 * LOG2E))
             if r0 == 0 and c0 + t == 0:
-                diagonal = on_diagonal(rows)
-                e = jnp.where(diagonal, 0.0, e)
-                same = same & ~diagonal
-            w[at, here] = e
+                e = jnp.where(on_diagonal(rows), 0.0, e)
             cs[:, here] += jnp.sum(e.reshape(rows // 8, 8, 128), axis=0)
-            ps = jnp.where(same, s, 0.0)
-            if t == 0:
-                total, positive = e, ps
-            else:
-                total, positive = total + e, positive + ps
+            total = e if t == 0 else total + e
         est[at, :] += total
-        pst[at, :] += positive
+
+    def positives():
+        for r in range(0, ANCHORS, 32):
+            at = pl.ds(r, 32)
+            label = labc[at, :]
+            total = jnp.zeros((32, 128), F32)
+            for c in range(0, KEYS, 128):
+                here = pl.ds(c, 128)
+                same = label == klab[0:1, here]
+                if c == 0 and r < BLOCK:
+                    i = lax.broadcasted_iota(jnp.int32, (32, 128), 0) + r
+                    same = same & (i != lax.broadcasted_iota(jnp.int32, (32, 128), 1))
+                total = total + jnp.where(same, w[at, here], 0.0)
+            pst[at, :] = total
 
     def need(r0, rows, c0, cols):
         wants = set()
@@ -296,31 +298,26 @@
                     wants |= {("S" if s else "K", dq, dp, h) for h in range(PIECES)}
         return wants
 
-    work = [("count", r) for r in range(0, ANCHORS, 192)]
+    work = []
     for r0, rows, c0, c1, wide in (
         (0, 288, 0, GROUP, 256),
         (288, 192, 0, GROUP, 256),
         (0, 480, GROUP, 2 * GROUP, 256),
         (480, 192, 0, 2 * GROUP, 256),
         (0, 672, 2 * GROUP, 3 * GROUP, 256),
-        (0, 672, 3 * GROUP, 3 * GROUP + 512, 256),
         (672, 96, 0, 3 * GROUP, GROUP),
-        (0, 672, 3 * GROUP + 512, 4 * GROUP, 256),
-        (672, 96, 3 * GROUP, 4 * GROUP, GROUP),
+        (0, 768, 3 * GROUP, 4 * GROUP, 256),
     ):
         work += [(r0, rows, c, wide) for c in range(c0, c1, wide)]
-    work.insert(10, ("done",))
-
     seen = set()
 
     def receive(what):
         if what in seen:
             return
         seen.add(what)
-        if what[0] == "A":
-            arrived(what, a_ref(what[1], what[2]))
-        else:
-            arrived(what, k_ref(1 if what[0] == "S" else 0, *what[1:]))
+        if what[-1] == 0:
+            arrived(("L",) + what, line_place(what))
+        arrived(what, place(what))
         if what[0] != "S":
             hand_on(what)
 
@@ -328,25 +325,19 @@
         return all(v in seen for v in wants if v[0] != "S")
 
     def do(job):
-        if job[0] == "count":
-            count(job[1])
-        elif job[0] == "done":
-            counts_ready()
-        else:
-            for v in sorted(need(*job) - seen):
-                receive(v)
-            score(*job)
+        for v in sorted(need(*job) - seen):
+            receive(v)
+        score(*job)
 
     left = list(range(len(work)))
     for n, what in enumerate(ARRIVALS):
         receive(what)
-        if n == LABELS_AT:
-            labels_ready()
         for i in JOBS_AFTER.get(n, ()):
             do(work[i])
             left.remove(i)
     for i in left:
         do(work[i])
+    assert len(seen) == PIECES * (N_Z - 1 + 15 + 16)
 
     tiles = [jnp.sum(cs[:, t * 128 : (t + 1) * 128], axis=0, keepdims=True) for t in range(KEYS // 128)]
     for s in (0, 1):
@@ -362,6 +353,7 @@
     post(("X",), kso, ksi, chip(0, 0, True))
     lines(est, eto)
     exchange("E", eto, eti)
+    labels_ready()
     arrived(("X",), ksi)
     both = [kso[0:16, :] + ksi[16:32, :], kso[16:32, :] + ksi[0:16, :]]
     kvo[0:16, :] = both[0].astype(BF16)
@@ -369,12 +361,15 @@
     plane = [(dq, dp) for dq, dp in reversed(K_ORDER) if (dq, dp) != (0, 0)]
     for dq, dp in plane:
         post(("V", dq, dp), kvo, kvi.at[dq * 4 + dp], chip(-dp, -dq, False))
+    count()
+    positives()
     real = lane < BLOCK
     totals = jnp.where(real, gathered("E", eto, eti), 1.0)
     inverse_total = 1.0 / totals
     columns(inverse_total, iec)
+    counts_ready()
     share = jnp.sum(pst[0:ANCHORS, :] * idc[...], axis=0, keepdims=True) * -5.0
-    tail = jnp.where(real, eio[...] * (jnp.log(totals[0:1]) + 10.0), 0.0)
+    tail = jnp.where(real, eio[...] * jnp.log(totals[0:1]), 0.0)
     lz[...] = share + tail
     for dz in range(1, N_Z):
         post(("P", 8 - dz), lz, lzi.at[8 - dz], up(dz))
@@ -414,10 +409,12 @@
             for c in range(0, KEYS, 128):
                 here = pl.ds(c, 128)
                 same = label == klab[0:1, here]
+                e = jnp.exp2(w[at, here] * (10.0 * LOG2E))
                 if c == 0 and r < BLOCK:
                     i = lax.broadcasted_iota(jnp.int32, (16, 128), 0) + r
-                    same = same & (i != lax.broadcasted_iota(jnp.int32, (16, 128), 1))
-                v = w[at, here] * (ie + kie[0:1, here]) - jnp.where(same, d2, 0.0)
+                    other = i != lax.broadcasted_iota(jnp.int32, (16, 128), 1)
+                    same, e = same & other, jnp.where(other, e, 0.0)
+                v = e * (ie + kie[0:1, here]) - jnp.where(same, d2, 0.0)
                 cm[at, here] = v.astype(BF16)
 
     def product(j, r0, rows):
@@ -513,7 +510,6 @@
         ((CHUNKS, ANCHORS, WIDE), F32),
         ((BLOCK, DEPTH), F32),
         ((BLOCK, 128), F32),
-        ((4, 1, 128), F32),
         ((N_Z, 1, 128), F32),
         ((32, 1, 128), F32),
         ((ANCHORS, 128), F32),

time: 72.1 us -> 71.7 us (level)
  no operation moved by 1% of the time
where the time goes in v5:
time: 71.7 us; the launch traced here: 71.6 us
  Pallas kernels  69.1 us (96%)
  between operations  1.81 us (3%)
  local copies, waits for them, and re-layouts  0.75 us (1%)
    pallas_call x1, Pallas kernels, per_device(): pl.pallas_call(kernel, out_shape=(pltpu.VMEM((BLOCK, DEPTH), F32), jax.Sh...  69.1 us

profile of v5, /device:TPU:1, one launch (start us, length us, event | category | flops | bytes accessed | tf_op | source)
XLA Modules:
  0.0 71.6 jit_solution(1498535574538241071)
XLA Ops:
  0.6 69.1 %shard_map.41 = (f32[96,1024]{1,0:T(8,128)S(1)}, f32[1,128]{1,0:T(1,128)}) custom-call(bf16[96,1024]{1,0:T(8,128)(2,1)} %emb.1, s32[1,96]{1,0:T(1,128)} %bitcast.3), custom_call_target="tpu_custom_call" | custom-call | flops 9663676416 | bytes 1048576 | tf_op jit(solution)/shard_map/pallas_call | solution.py:540
  69.7 0.0 copy-start
  69.7 0.7 %copy.6 = f32[96,1024]{1,0:T(8,128)} copy(f32[96,1024]{1,0:T(8,128)S(1)} %get-tuple-element.6) | data formatting | bytes 786432
  70.5 0.0 copy-done
Async XLA Ops:
  69.7 0.8 %copy-start = (f32[1,128]{1,0:T(1,128)S(1)}, f32[1,128]{1,0:T(1,128)}, u32[]{:S(2)}) copy-start(f32[1,128]{1,0:T(1,128)} %get-tuple-element.5) | copy-start | bytes 1540

commit v6 on v4

--- a/solution.py
+++ b/solution.py
@@ -48,7 +48,7 @@
 ]
 LABELS_AT = 17
 JOBS_AFTER = {
-    17: (0,), 18: (1, 2), 21: (3, 4), 25: (5,), 26: (6,), 36: (7, 8, 9, 11), 41: (12, 13), 44: (10,), 58: (14,), 59: (15, 16, 17), 60: (18, 19, 20), 61: (21, 22), 62: (23, 24),
+    17: (0,), 18: (1, 2), 21: (3, 4), 25: (5,), 26: (6,), 36: (7, 8, 9, 11), 41: (12, 13), 44: (10,), 58: (14,), 59: (15, 16, 17), 60: (18, 19, 20), 61: (21, 22),
 }
 
 
@@ -102,6 +102,11 @@
         copy.start()
         pending.append(copy)
 
+    def sent(n):
+        for copy in pending[:n]:
+            copy.wait_send()
+        del pending[:n]
+
     def arrived(name, dst):
         message(name, dst, dst, up(1)).wait_recv()
 
@@ -124,7 +129,6 @@
     fetch_line = pltpu.make_async_copy(lab, own_line, load.at[1])
     fetch_line.start()
     est[...] = jnp.zeros_like(est)
-    pst[...] = jnp.zeros_like(pst)
     cst[...] = jnp.zeros_like(cst)
     cs[...] = jnp.zeros_like(cs)
     al[0] = jnp.zeros((1, 128), F32)
@@ -263,26 +267,31 @@
     def score(r0, rows, c0, cols):
         at = pl.ds(r0, rows)
         acc = lax.dot_general(au[at, :], ku[pl.ds(c0, cols), :], NT, preferred_element_type=F32)
-        label = labc[at, :]
-        total = positive = None
+        total = None
         for t in range(cols // 128):
             here = pl.ds(c0 + t * 128, 128)
             s = acc[:, t * 128 : (t + 1) * 128]
-            e = jnp.exp2(s * (10.0 * LOG2E) - 10.0 * LOG2E)
-            same = label == klab[0:1, here]
+            w[at, here] = s
+            e = jnp.exp2(s * (10.0 * LOG2E))
             if r0 == 0 and c0 + t == 0:
-                diagonal = on_diagonal(rows)
-                e = jnp.where(diagonal, 0.0, e)
-                same = same & ~diagonal
-            w[at, here] = e
+                e = jnp.where(on_diagonal(rows), 0.0, e)
             cs[:, here] += jnp.sum(e.reshape(rows // 8, 8, 128), axis=0)
-            ps = jnp.where(same, s, 0.0)
-            if t == 0:
-                total, positive = e, ps
-            else:
-                total, positive = total + e, positive + ps
+            total = e if t == 0 else total + e
         est[at, :] += total
-        pst[at, :] += positive
+
+    def positives():
+        for r in range(0, ANCHORS, 32):
+            at = pl.ds(r, 32)
+            label = labc[at, :]
+            total = jnp.zeros((32, 128), F32)
+            for c in range(0, KEYS, 128):
+                here = pl.ds(c, 128)
+                same = label == klab[0:1, here]
+                if c == 0 and r < BLOCK:
+                    i = lax.broadcasted_iota(jnp.int32, (32, 128), 0) + r
+                    same = same & (i != lax.broadcasted_iota(jnp.int32, (32, 128), 1))
+                total = total + jnp.where(same, w[at, here], 0.0)
+            pst[at, :] = total
 
     def need(r0, rows, c0, cols):
         wants = set()
@@ -303,10 +312,8 @@
         (0, 480, GROUP, 2 * GROUP, 256),
         (480, 192, 0, 2 * GROUP, 256),
         (0, 672, 2 * GROUP, 3 * GROUP, 256),
-        (0, 672, 3 * GROUP, 3 * GROUP + 512, 256),
         (672, 96, 0, 3 * GROUP, GROUP),
-        (0, 672, 3 * GROUP + 512, 4 * GROUP, 256),
-        (672, 96, 3 * GROUP, 4 * GROUP, GROUP),
+        (0, 768, 3 * GROUP, 4 * GROUP, 256),
     ):
         work += [(r0, rows, c, wide) for c in range(c0, c1, wide)]
     work.insert(10, ("done",))
@@ -348,6 +355,7 @@
     for i in left:
         do(work[i])
 
+    gathered_by = len(pending)
     tiles = [jnp.sum(cs[:, t * 128 : (t + 1) * 128], axis=0, keepdims=True) for t in range(KEYS // 128)]
     for s in (0, 1):
         for dq, dp in K_ORDER:
@@ -373,8 +381,10 @@
     totals = jnp.where(real, gathered("E", eto, eti), 1.0)
     inverse_total = 1.0 / totals
     columns(inverse_total, iec)
+    positives()
+    sent(gathered_by)
     share = jnp.sum(pst[0:ANCHORS, :] * idc[...], axis=0, keepdims=True) * -5.0
-    tail = jnp.where(real, eio[...] * (jnp.log(totals[0:1]) + 10.0), 0.0)
+    tail = jnp.where(real, eio[...] * jnp.log(totals[0:1]), 0.0)
     lz[...] = share + tail
     for dz in range(1, N_Z):
         post(("P", 8 - dz), lz, lzi.at[8 - dz], up(dz))
@@ -414,10 +424,12 @@
             for c in range(0, KEYS, 128):
                 here = pl.ds(c, 128)
                 same = label == klab[0:1, here]
+                e = jnp.exp2(w[at, here] * (10.0 * LOG2E))
                 if c == 0 and r < BLOCK:
                     i = lax.broadcasted_iota(jnp.int32, (16, 128), 0) + r
-                    same = same & (i != lax.broadcasted_iota(jnp.int32, (16, 128), 1))
-                v = w[at, here] * (ie + kie[0:1, here]) - jnp.where(same, d2, 0.0)
+                    other = i != lax.broadcasted_iota(jnp.int32, (16, 128), 1)
+                    same, e = same & other, jnp.where(other, e, 0.0)
+                v = e * (ie + kie[0:1, here]) - jnp.where(same, d2, 0.0)
                 cm[at, here] = v.astype(BF16)
 
     def product(j, r0, rows):
@@ -462,18 +474,20 @@
     for j in range(CHUNKS):
         product(j, 96, 192)
     coupling(0, 96)
-    for j in range(CHUNKS):
-        push(j, 2)
-        product(j, 0, 96)
     whole = lz[...]
     for dz in range(1, N_Z):
         arrived(("P", dz), lzi.at[dz])
         whole = whole + lzi[dz]
     lo[...] = whole
-    for s, dq, dp in peers:
-        post(("W", s, dq, dp), lo, li.at[key_slot(s, dq, dp)], chip(-dp, -dq, s))
+    before = len(pending)
+    for j in range(CHUNKS):
+        push(j, 2)
+        product(j, 0, 96)
+        for s, dq, dp in peers[j::CHUNKS]:
+            post(("W", s, dq, dp), lo, li.at[key_slot(s, dq, dp)], chip(-dp, -dq, s))
     for j in range(CHUNKS):
         push(j, 3)
+    sent(before)
 
     every = lo[...]
     for s, dq, dp in peers:
@@ -481,6 +495,7 @@
         every = every + li[key_slot(s, dq, dp)]
     loss[...] = jnp.broadcast_to(jnp.sum(every, axis=1, keepdims=True) * (1.0 / TOKENS), (1, 128))
 
+    sent(len(pending) - 2 * CHUNKS)
     along = jnp.zeros((BLOCK, 1), F32)
     for j in range(CHUNKS):
         value = part(j, 0, 0, BLOCK)
@@ -495,8 +510,7 @@
         cut = slice(j * WIDE, (j + 1) * WIDE)
         grad[:, cut] = (g[j, pl.ds(0, BLOCK), :] - uf[:, cut] * along) * scale
 
-    for copy in pending:
-        copy.wait_send()
+    sent(len(pending))
     assert len(number.numbers) <= N_SEM
 
 

time: 72.1 us -> 70 us (0.971)
  Pallas kernels: 69.5 us -> 67.3 us
    pallas_call x1, Pallas kernels: 69.5 us -> 67.3 us  [per_device(): pl.pallas_call(kernel, out_shape=(pltpu.VMEM((BLOCK, DEPTH), F32), jax.Sh...]
where the time goes in v6:
time: 70 us; the launch traced here: 69.9 us
  Pallas kernels  67.3 us (96%)
  between operations  1.81 us (3%)
  local copies, waits for them, and re-layouts  0.75 us (1%)
    pallas_call x1, Pallas kernels, per_device(): pl.pallas_call(kernel, out_shape=(pltpu.VMEM((BLOCK, DEPTH), F32), jax.Sh...  67.3 us

profile of v6, /device:TPU:1, one launch (start us, length us, event | category | flops | bytes accessed | tf_op | source)
XLA Modules:
  0.0 69.9 jit_solution(1092995064177825864)
XLA Ops:
  0.6 67.3 %shard_map.41 = (f32[96,1024]{1,0:T(8,128)S(1)}, f32[1,128]{1,0:T(1,128)}) custom-call(bf16[96,1024]{1,0:T(8,128)(2,1)} %emb.1, s32[1,96]{1,0:T(1,128)} %bitcast.3), custom_call_target="tpu_custom_call" | custom-call | flops 9663676416 | bytes 1048576 | tf_op jit(solution)/shard_map/pallas_call | solution.py:558
  68.0 0.0 copy-start
  68.0 0.7 %copy.6 = f32[96,1024]{1,0:T(8,128)} copy(f32[96,1024]{1,0:T(8,128)S(1)} %get-tuple-element.6) | data formatting | bytes 786432
  68.7 0.0 copy-done
Async XLA Ops:
  68.0 0.8 %copy-start = (f32[1,128]{1,0:T(1,128)S(1)}, f32[1,128]{1,0:T(1,128)}, u32[]{:S(2)}) copy-start(f32[1,128]{1,0:T(1,128)} %get-tuple-element.5) | copy-start | bytes 1540

commit v7 on v6

--- a/solution.py
+++ b/solution.py
@@ -377,12 +377,12 @@
     plane = [(dq, dp) for dq, dp in reversed(K_ORDER) if (dq, dp) != (0, 0)]
     for dq, dp in plane:
         post(("V", dq, dp), kvo, kvi.at[dq * 4 + dp], chip(-dp, -dq, False))
+    positives()
+    sent(gathered_by)
     real = lane < BLOCK
     totals = jnp.where(real, gathered("E", eto, eti), 1.0)
     inverse_total = 1.0 / totals
     columns(inverse_total, iec)
-    positives()
-    sent(gathered_by)
     share = jnp.sum(pst[0:ANCHORS, :] * idc[...], axis=0, keepdims=True) * -5.0
     tail = jnp.where(real, eio[...] * jnp.log(totals[0:1]), 0.0)
     lz[...] = share + tail

time: 70 us -> 70.8 us (1.011)
  Pallas kernels: 67.3 us -> 68.2 us
    pallas_call x1, Pallas kernels: 67.3 us -> 68.2 us  [per_device(): pl.pallas_call(kernel, out_shape=(pltpu.VMEM((BLOCK, DEPTH), F32), jax.Sh...]
where the time goes in v7:
time: 70.8 us; the launch traced here: 70.7 us
  Pallas kernels  68.2 us (96%)
  between operations  1.81 us (3%)
  local copies, waits for them, and re-layouts  0.75 us (1%)
    pallas_call x1, Pallas kernels, per_device(): pl.pallas_call(kernel, out_shape=(pltpu.VMEM((BLOCK, DEPTH), F32), jax.Sh...  68.2 us

profile of v7, /device:TPU:1, one launch (start us, length us, event | category | flops | bytes accessed | tf_op | source)
XLA Modules:
  0.0 70.7 jit_solution(7640763616724190156)
XLA Ops:
  0.6 68.2 %shard_map.41 = (f32[96,1024]{1,0:T(8,128)S(1)}, f32[1,128]{1,0:T(1,128)}) custom-call(bf16[96,1024]{1,0:T(8,128)(2,1)} %emb.1, s32[1,96]{1,0:T(1,128)} %bitcast.3), custom_call_target="tpu_custom_call" | custom-call | flops 9663676416 | bytes 1048576 | tf_op jit(solution)/shard_map/pallas_call | solution.py:558
  68.8 0.0 copy-start
  68.8 0.7 %copy.6 = f32[96,1024]{1,0:T(8,128)} copy(f32[96,1024]{1,0:T(8,128)S(1)} %get-tuple-element.6) | data formatting | bytes 786432
  69.6 0.0 copy-done
Async XLA Ops:
  68.8 0.8 %copy-start = (f32[1,128]{1,0:T(1,128)S(1)}, f32[1,128]{1,0:T(1,128)}, u32[]{:S(2)}) copy-start(f32[1,128]{1,0:T(1,128)} %get-tuple-element.5) | copy-start | bytes 1540

commit v8 on v6

--- a/solution.py
+++ b/solution.py
@@ -382,7 +382,6 @@
     inverse_total = 1.0 / totals
     columns(inverse_total, iec)
     positives()
-    sent(gathered_by)
     share = jnp.sum(pst[0:ANCHORS, :] * idc[...], axis=0, keepdims=True) * -5.0
     tail = jnp.where(real, eio[...] * jnp.log(totals[0:1]), 0.0)
     lz[...] = share + tail
@@ -473,6 +472,7 @@
     coupling(96, 192)
     for j in range(CHUNKS):
         product(j, 96, 192)
+    sent(gathered_by)
     coupling(0, 96)
     whole = lz[...]
     for dz in range(1, N_Z):

time: 70 us -> 70.8 us (1.011)
  Pallas kernels: 67.3 us -> 68.1 us
    pallas_call x1, Pallas kernels: 67.3 us -> 68.1 us  [per_device(): pl.pallas_call(kernel, out_shape=(pltpu.VMEM((BLOCK, DEPTH), F32), jax.Sh...]
where the time goes in v8:
time: 70.8 us; the launch traced here: 70.7 us
  Pallas kernels  68.1 us (96%)
  between operations  1.81 us (3%)
  local copies, waits for them, and re-layouts  0.75 us (1%)
    pallas_call x1, Pallas kernels, per_device(): pl.pallas_call(kernel, out_shape=(pltpu.VMEM((BLOCK, DEPTH), F32), jax.Sh...  68.1 us

profile of v8, /device:TPU:1, one launch (start us, length us, event | category | flops | bytes accessed | tf_op | source)
XLA Modules:
  0.0 70.7 jit_solution(14434247959131232705)
XLA Ops:
  0.6 68.1 %shard_map.41 = (f32[96,1024]{1,0:T(8,128)S(1)}, f32[1,128]{1,0:T(1,128)}) custom-call(bf16[96,1024]{1,0:T(8,128)(2,1)} %emb.1, s32[1,96]{1,0:T(1,128)} %bitcast.3), custom_call_target="tpu_custom_call" | custom-call | flops 9663676416 | bytes 1048576 | tf_op jit(solution)/shard_map/pallas_call | solution.py:558
  68.7 0.0 copy-start
  68.8 0.7 %copy.6 = f32[96,1024]{1,0:T(8,128)} copy(f32[96,1024]{1,0:T(8,128)S(1)} %get-tuple-element.6) | data formatting | bytes 786432
  69.5 0.0 copy-done
Async XLA Ops:
  68.7 0.8 %copy-start = (f32[1,128]{1,0:T(1,128)S(1)}, f32[1,128]{1,0:T(1,128)}, u32[]{:S(2)}) copy-start(f32[1,128]{1,0:T(1,128)} %get-tuple-element.5) | copy-start | bytes 1540
